TPU v7x, 32 devices: a whole 2x2x4 slice. The times are simulated.
32 devices in a mesh: img: 8 (over y, x, core), slab: 4 (over z).
Axes of the slice: x: 2, y: 2, z: 4, core: 2. Of those that a mesh axis runs over, the one named last changes fastest.
Arguments:
- state: float32 [64, 2, 128, 4, 128], P('img', None, 'slab'), may hold values from -3 to 3
- sources: int32 [64, 2], replicated, may hold values from 0 to 63, as said below
- weight_index: int32 [64], P('img'), may hold values from 0 to 15
Outputs:
- moved: float32 [64, 2, 128, 4, 128], P('img', None, 'slab')
Inputs may be any that keep to these rules, and one draw needn't show every extreme that they name: Among the 16 sources of the 8 new images of one device (aligned blocks), at most 2 lie among the 8 images of any one device, and in every draw exactly 2 do for some devices.
All inputs are finite; a program needn't handle non-finite values.
Results may differ from a plain program's by a relative error of at most 0.00022.
Values sent between devices are 32-bit elements; how exact they have to be, the bound alone decides.
A program may use at most 128 MiB of HBM per device.

v0:
```python
import jax
import jax.numpy as jnp
from jax import lax
from jax.sharding import PartitionSpec as P

WLEVELS = 16


KAPPA = 0.25
COUPLE = 0.3
STEP_SIZE = 0.004
EPSILON = 1e-06


def with_halo(block, sides, width):
    for axis, dim in sides:
        count = lax.axis_size(axis)
        forward = [(i, i + 1) for i in range(count - 1)]
        backward = [(target, source) for source, target in forward]
        low = lax.ppermute(
            lax.slice_in_dim(block, block.shape[dim] - width, None, axis=dim), axis, forward
        )
        high = lax.ppermute(lax.slice_in_dim(block, 0, width, axis=dim), axis, backward)
        block = jnp.concatenate([low, block, high], axis=dim)
    return block


def drift(phi, face):
    padded = jnp.pad(phi, ((0, 0), (1, 1), (0, 0), (0, 0)))
    lapl = padded[:, 2:] + padded[:, :-2]
    lapl = lapl + jnp.roll(phi, 1, 2) + jnp.roll(phi, -1, 2)
    lapl = lapl + jnp.roll(phi, 1, 3) + jnp.roll(phi, -1, 3) - 6.0 * phi
    potential = phi * phi * phi - phi + COUPLE * phi[::-1] - KAPPA * lapl
    mobile = 0.5 + 1.0 / (1.0 + phi * phi)
    total = jnp.zeros_like(phi)
    for axis_no in (2, 3):
        face_mob = 0.5 * (mobile + jnp.roll(mobile, -1, axis_no))
        flux = face_mob * (jnp.roll(potential, -1, axis_no) - potential)
        total = total + flux - jnp.roll(flux, 1, axis_no)
    face_z = 0.5 * (mobile[:, 1:] + mobile[:, :-1]) * face[None, :, None, None]
    flux_z = face_z * (potential[:, 1:] - potential[:, :-1])
    total = total + jnp.pad(flux_z, ((0, 0), (0, 1), (0, 0), (0, 0)))
    total = total - jnp.pad(flux_z, ((0, 0), (1, 0), (0, 0), (0, 0)))
    return total


def face_mask(zbase, total_z, depth, margin):
    rows = zbase - margin + jnp.arange(depth + 2 * margin, dtype=jnp.int32)
    inside = (rows >= 0) & (rows < total_z)
    return ((inside[1:] & inside[:-1]).astype(jnp.float32), inside)


def pull_back(window, moment, face):

    def single(pair):
        field, cotangent = pair
        _, back = jax.vjp(lambda value: drift(value, face), field)
        return back(cotangent)[0]

    return lax.map(single, (window, moment))


def all_drifts(window, face):
    return lax.map(lambda field: drift(field, face), window)


def scales(own_drift, tangent):
    drift_sq, tangent_sq = lax.psum(
        (
            jnp.sum(own_drift * own_drift, axis=(1, 2, 3, 4)),
            jnp.sum(tangent * tangent, axis=(1, 2, 3, 4)),
        ),
        "slab",
    )
    return jnp.sqrt(drift_sq) / jnp.sqrt(tangent_sq + EPSILON)


def local(state, sources, weight_index):
    count = lax.axis_size("img")
    img_rank = lax.axis_index("img")
    per_dev = state.shape[0]
    images = per_dev * count
    depth = state.shape[2]
    total_z = depth * lax.axis_size("slab")
    zbase = lax.axis_index("slab") * depth
    path = with_halo(state, (("img", 0),), 1)
    tangent = (path[2:] - path[:-2]) * ((images - 1) / 2.0)
    second = (path[2:] - 2.0 * path[1:-1] + path[:-2]) * float((images - 1) ** 2)
    window = with_halo(state, (("slab", 2),), 3)
    face, inside = face_mask(zbase, total_z, depth, 3)
    drifts = all_drifts(window, face)
    own_drift = drifts[:, :, 3:-3]
    scale = scales(own_drift, tangent)
    moment = scale[:, None, None, None, None] * tangent - own_drift
    moment_rim = with_halo(moment, (("slab", 2),), 2)
    moment_rim = jnp.pad(moment_rim, ((0, 0), (0, 0), (1, 1), (0, 0), (0, 0)))
    pulled = pull_back(window, moment_rim, face)[:, :, 3:-3]
    global_ids = img_rank * per_dev + jnp.arange(per_dev, dtype=jnp.int32)
    interior = ((global_ids > 0) & (global_ids < images - 1))[:, None, None, None, None]
    square = (scale * scale)[:, None, None, None, None]
    updated = jnp.where(interior, state + STEP_SIZE * (square * second + pulled), state)
    weights = (weight_index.astype(jnp.float32) + 1.0) / (WLEVELS + 1.0)
    mine = lax.dynamic_slice_in_dim(sources, img_rank * per_dev, per_dev, 0)
    piece = lax.all_gather(updated, "img", axis=0, tiled=True)
    number = piece.shape[0]
    image_ids = jnp.arange(number, dtype=jnp.int32)
    table = weights[:, None] * (mine[:, 0:1] == image_ids[None, :]).astype(jnp.float32)
    table = table + (1.0 - weights)[:, None] * (mine[:, 1:2] == image_ids[None, :]).astype(
        jnp.float32
    )
    flat = piece.reshape(number, -1)
    added = jnp.dot(
        table, flat, precision=lax.Precision.HIGHEST, preferred_element_type=jnp.float32
    )
    return added.reshape(jnp.zeros_like(updated).shape)


def solution(mesh):
    return jax.shard_map(
        local,
        mesh=mesh,
        in_specs=(P("img", None, "slab", None, None), P(), P("img")),
        out_specs=P("img", None, "slab", None, None),
        check_vma=False,
    )
```

profile of v0, /device:TPU:0, one launch (start us, length us, event | category | flops | bytes accessed | tf_op | source)
XLA Modules:
  0.0 224.1 jit_solution(17353783476429485410)
XLA Ops:
  6.5 1.4 copy.27
  8.7 1.3 collective-permute-start
  10.0 3.7 %collective-permute-start.1 = (f32[1,2,32,4,128]{4,2,3,1,0:T(8,128)}, f32[1,2,32,4,128]{4,2,3,1,0:T(8,128)}, u32[]{:S(2)}, u32[]{:S(2)}) collective-permute-start(f32[1,2,32,4,128]{4,2,3,1,0:T(8,128)} %get-tuple-element.205), channel_id=1, source_target_pairs={{0,4},{4,8},{8,12},{12,16},{16,20},{20,24},{24,28},{1,5},{5,9},{9,... | collective-permute-start | bytes 393224 | tf_op jit(solution)/shard_map/ppermute | solution.py:20
  14.4 4.9 %collective-permute-start.2 = (f32[8,2,3,4,128]{4,3,2,1,0:T(4,128)S(1)}, f32[8,2,3,4,128]{4,3,2,1,0:T(4,128)S(1)}, u32[]{:S(2)}, u32[]{:S(2)}) collective-permute-start(f32[8,2,3,4,128]{4,3,2,1,0:T(4,128)S(1)} %get-tuple-element.207), channel_id=1, source_target_pairs={{0,1},{1,2},{2,3},{4,5},{5,6},{6,7},{8,9},{9,10},{10,11},{12,13},{... | collective-permute-start | bytes 294920 | tf_op jit(solution)/shard_map/ppermute | solution.py:20
  19.3 1.3 collective-permute-start.3
  20.7 1.3 collective-permute-done.2
  22.1 4.2 %collective-permute-done.3 = f32[8,2,3,4,128]{4,3,2,1,0:T(4,128)S(1)} collective-permute-done((f32[8,2,3,4,128]{4,3,2,1,0:T(4,128)}, f32[8,2,3,4,128]{4,3,2,1,0:T(4,128)S(1)}, u32[]{:S(2)}, u32[]{:S(2)}) %collective-permute-start.3) | collective-permute-done | bytes 98336 | tf_op jit(solution)/shard_map/ppermute | solution.py:23
  26.5 18.8 %while.24 = (s32[]{:T(128)}, f32[8,2,38,4,128]{4,3,2,1,0:T(4,128)S(1)}, f32[8,2,38,4,128]{4,3,2,1,0:T(4,128)S(1)}, f32[37]{0:T(128)S(1)}, s32[]{:T(128)}) while((s32[]{:T(128)}, f32[8,2,38,4,128]{4,3,2,1,0:T(4,128)S(1)}, f32[8,2,38,4,128]{4,3,2,1,0:T(4,128)S(1)}, f32[37]{0:T(128)S(1)}, s32[]{:T(128)}) %tuple.116), condition=%wide.region_1.2_spmd, body=%wide.region_0.1_spmd.sunk | while | flops 1902631 | bytes 7094401 | solution.py:64
  46.3 1.0 copy-done.3
  47.4 1.4 copy.24
  49.0 1.2 multiply_reduce_fusion
  50.2 10.0 %all-reduce.31 = (f32[8]{0:T(128)S(1)}, f32[8]{0:T(128)S(1)}) all-reduce(f32[8]{0:T(128)S(1)} %multiply_reduce_fusion, f32[8]{0:T(128)S(1)} %multiply_reduce_fusion.1), channel_id=1, replica_groups=mesh['img'=8,'slab'=4] {'slab'}, use_global_device_ids=true, to_apply=%region_5.6 | all-reduce | flops 16 | bytes 128 | tf_op jit(solution)/shard_map/psum | solution.py:68
  60.3 1.3 multiply_subtract_fusion.2
  61.6 2.4 %collective-permute-start.4 = (f32[8,2,2,4,128]{4,2,3,1,0:T(2,128)S(1)}, f32[8,2,2,4,128]{4,2,3,1,0:T(2,128)S(1)}, u32[]{:S(2)}, u32[]{:S(2)}) collective-permute-start(f32[8,2,2,4,128]{4,2,3,1,0:T(2,128)S(1)} %get-tuple-element.202), channel_id=1, source_target_pairs={{0,1},{1,2},{2,3},{4,5},{5,6},{6,7},{8,9},{9,10},{10,11},{12,13},{... | collective-permute-start | bytes 196616 | tf_op jit(solution)/shard_map/ppermute | solution.py:20
  64.1 1.3 collective-permute-start.5
  66.0 4.3 %collective-permute-done.5 = f32[8,2,2,4,128]{4,2,3,1,0:T(2,128)S(1)} collective-permute-done((f32[8,2,2,4,128]{4,2,3,1,0:T(2,128)S(1)}, f32[8,2,2,4,128]{4,2,3,1,0:T(2,128)S(1)}, u32[]{:S(2)}, u32[]{:S(2)}) %collective-permute-start.5) | collective-permute-done | bytes 65568 | tf_op jit(solution)/shard_map/ppermute | solution.py:23
  71.2 41.1 %while.25 = (s32[]{:T(128)}, f32[8,2,38,4,128]{4,3,2,1,0:T(4,128)S(1)}, f32[8,2,38,4,128]{4,3,2,1,0:T(4,128)}, f32[8,2,38,4,128]{4,3,2,1,0:T(4,128)S(1)}, f32[37]{0:T(128)S(1)}, /*index=5*/s32[]{:T(128)}) while((s32[]{:T(128)}, f32[8,2,38,4,128]{4,3,2,1,0:T(4,128)S(1)}, f32[8,2,38,4,128]{4,3,2,1,0:T(4,128)}, ...), condition=%wide.region_7.8_spmd, body=%wide.region_6.7_spmd.sunk | while | flops 4076583 | bytes 13607197 | solution.py:60
  112.4 2.4 %add_select_fusion = f32[8,2,32,4,128]{4,2,3,1,0:T(8,128)} fusion(f32[8,2,32,4,128]{4,2,3,1,0:T(8,128)S(1)} %copy.27, f32[8,2,38,4,128]{4,2,3,1,0:T(8,128)S(1)} %copy.26, f32[1,2,32,4,128]{4,2,3,1,0:T(8,128)} %collective-permute-done, f32[1,2,32,4,128]{4,2,3,1,0:T(8,128)} %collective-permute-done.1, f32[8]{0:T(128)S(1)} %get-tuple-element.165, ...), kind=kLoop, calls=%fused_computation.88 | loop fusion | flops 2621440 | bytes 3407912 | tf_op jit(solution)/shard_map/jit(_where)/select_n | solution.py:101
  114.9 52.4 %all-gather.2.cloned.1.call-done = f32[64,2,32,4,128]{4,2,3,1,0:T(8,128)} async-done(((f32[8,2,32,4,128]{4,2,3,1,0:T(8,128)}), f32[64,2,32,4,128]{4,2,3,1,0:T(8,128)}) %all-gather.2.cloned.1.call-update) | async-done | bytes 8388624 | tf_op jit(solution)/shard_map/all_gather | solution.py:104
  167.3 14.9 %copy.29 = f32[64,2,32,4,128]{4,3,2,1,0:T(4,128)} copy(f32[64,2,32,4,128]{4,2,3,1,0:T(8,128)} %all-gather.2.cloned.1.call-done) | data formatting | bytes 16777216 | tf_op jit(solution)/shard_map/all_gather | solution.py:104
  182.2 10.6 %reshape.18 = f32[64,32768]{1,0:T(8,128)} reshape(f32[64,2,32,4,128]{4,3,2,1,0:T(4,128)} %copy.29) | data formatting | bytes 16777216 | tf_op jit(solution)/shard_map/reshape | solution.py:111
  192.8 10.9 %dot_general.8 = f32[2,32,4,128,64]{3,2,1,0,4:T(4,128)} reshape(f32[32768,64]{0,1:T(8,128)} %bitcast.75) | data formatting | bytes 16777216 | tf_op jit(solution)/shard_map/dot_general | solution.py:112
  203.7 12.3 %fusion.49 = f32[8,2,32,4,128]{4,0,3,2,1:T(8,128)S(1)} fusion(f32[2,32,4,128,64]{3,2,1,0,4:T(4,128)} %dot_general.8, f32[8]{0:T(128)S(1)} %get-tuple-element.211, s32[8]{0:T(128)S(1)} %get-tuple-element.209, f32[8]{0:T(128)S(1)} %get-tuple-element.210, s32[8]{0:T(128)S(1)} %get-tuple-element.208), kind=kOutput, calls=%fused_computation.86 | convolution fusion | flops 201329152 | bytes 9437312 | tf_op jit(solution)/shard_map/dot_general | solution.py:112
  216.0 1.2 copy.31
  (403 shorter events, 62.1 us)
Async XLA Ops:
  6.5 108.2 %copy-start = (s32[64,2]{0,1:T(2,128)S(1)}, s32[64,2]{0,1:T(2,128)}, u32[]{:S(2)}) copy-start(s32[64,2]{0,1:T(2,128)} %param.8) | copy-start | bytes 1540
  6.5 7.2 %copy-start.1 = (f32[8,2,32,4,128]{4,3,2,1,0:T(4,128)S(1)}, f32[8,2,32,4,128]{4,3,2,1,0:T(4,128)}, u32[]{:S(2)}) copy-start(f32[8,2,32,4,128]{4,3,2,1,0:T(4,128)} %param.7) | copy-start | bytes 3145732
  6.5 160.8 %all-gather.2.cloned.1.call-start = ((), (), s32[]{:S(2)}) async-start(), calls=%async_computation | async-start | bytes 9437184 | tf_op jit(solution)/shard_map/all_gather | solution.py:104
  8.7 40.3 %collective-permute-start = (f32[1,2,32,4,128]{4,2,3,1,0:T(8,128)}, f32[1,2,32,4,128]{4,2,3,1,0:T(8,128)}, u32[]{:S(2)}, u32[]{:S(2)}) collective-permute-start(f32[1,2,32,4,128]{4,2,3,1,0:T(8,128)} %get-tuple-element.204), channel_id=1, source_target_pairs={{4,0},{8,4},{12,8},{16,12},{20,16},{24,20},{28,24},{5,1},{9,5},{13... | collective-permute-start | bytes 393224 | tf_op jit(solution)/shard_map/ppermute | solution.py:23
  10.0 39.0 %collective-permute-start.1 = (f32[1,2,32,4,128]{4,2,3,1,0:T(8,128)}, f32[1,2,32,4,128]{4,2,3,1,0:T(8,128)}, u32[]{:S(2)}, u32[]{:S(2)}) collective-permute-start(f32[1,2,32,4,128]{4,2,3,1,0:T(8,128)} %get-tuple-element.205), channel_id=1, source_target_pairs={{0,4},{4,8},{8,12},{12,16},{16,20},{20,24},{24,28},{1,5},{5,9},{9,... | collective-permute-start | bytes 393224 | tf_op jit(solution)/shard_map/ppermute | solution.py:20
  14.4 7.6 %collective-permute-start.2 = (f32[8,2,3,4,128]{4,3,2,1,0:T(4,128)S(1)}, f32[8,2,3,4,128]{4,3,2,1,0:T(4,128)S(1)}, u32[]{:S(2)}, u32[]{:S(2)}) collective-permute-start(f32[8,2,3,4,128]{4,3,2,1,0:T(4,128)S(1)} %get-tuple-element.207), channel_id=1, source_target_pairs={{0,1},{1,2},{2,3},{4,5},{5,6},{6,7},{8,9},{9,10},{10,11},{12,13},{... | collective-permute-start | bytes 294920 | tf_op jit(solution)/shard_map/ppermute | solution.py:20
  19.3 7.0 %collective-permute-start.3 = (f32[8,2,3,4,128]{4,3,2,1,0:T(4,128)}, f32[8,2,3,4,128]{4,3,2,1,0:T(4,128)S(1)}, u32[]{:S(2)}, u32[]{:S(2)}) collective-permute-start(f32[8,2,3,4,128]{4,3,2,1,0:T(4,128)} %get-tuple-element.206), channel_id=1, source_target_pairs={{1,0},{2,1},{3,2},{5,4},{6,5},{7,6},{9,8},{10,9},{11,10},{13,12},{... | collective-permute-start | bytes 294920 | tf_op jit(solution)/shard_map/ppermute | solution.py:23
  45.3 1.0 copy-start.2
  46.3 1.0 copy-start.3
  61.6 4.3 %collective-permute-start.4 = (f32[8,2,2,4,128]{4,2,3,1,0:T(2,128)S(1)}, f32[8,2,2,4,128]{4,2,3,1,0:T(2,128)S(1)}, u32[]{:S(2)}, u32[]{:S(2)}) collective-permute-start(f32[8,2,2,4,128]{4,2,3,1,0:T(2,128)S(1)} %get-tuple-element.202), channel_id=1, source_target_pairs={{0,1},{1,2},{2,3},{4,5},{5,6},{6,7},{8,9},{9,10},{10,11},{12,13},{... | collective-permute-start | bytes 196616 | tf_op jit(solution)/shard_map/ppermute | solution.py:20
  64.1 6.2 %collective-permute-start.5 = (f32[8,2,2,4,128]{4,2,3,1,0:T(2,128)S(1)}, f32[8,2,2,4,128]{4,2,3,1,0:T(2,128)S(1)}, u32[]{:S(2)}, u32[]{:S(2)}) collective-permute-start(f32[8,2,2,4,128]{4,2,3,1,0:T(2,128)S(1)} %get-tuple-element.203), channel_id=1, source_target_pairs={{1,0},{2,1},{3,2},{5,4},{6,5},{7,6},{9,8},{10,9},{11,10},{13,12},{... | collective-permute-start | bytes 196616 | tf_op jit(solution)/shard_map/ppermute | solution.py:23
  112.3 2.5 %copy-start.4 = (s32[8]{0:T(128)S(1)}, s32[8]{0:T(128)}, u32[]{:S(2)}) copy-start(s32[8]{0:T(128)} %param.9) | copy-start | bytes 100
Sparse Core Ops, SparseCore 0:
  114.9 52.3 all-gather.1
where the time goes:
time: 225 us; the launch traced here: 224 us
  local copies, waits for them, and re-layouts  68.2 us (30%)
  waiting for transfers between devices  62.7 us (28%)
  other arithmetic  39.7 us (18%)
  starting transfers between devices  14.9 us (7%)
  between operations  13.6 us (6%)
  matrix products  12.3 us (5%)
  blocking collectives  10 us (4%)
  loops' own time  2.63 us (1%)
    all_gather x1, waiting for transfers between devices, local(): piece = lax.all_gather(updated, 'img', axis=0, tiled=True)  52.4 us
    all_gather x1, local copies, waits for them, and re-layouts, local(): piece = lax.all_gather(updated, 'img', axis=0, tiled=True)  14.9 us
    dot_general x1, matrix products, local(): jnp.dot(table, flat, precision=lax.Precision.HIGHEST, preferred_element_t...  12.3 us
    dot_general x2, local copies, waits for them, and re-layouts, local(): jnp.dot(table, flat, precision=lax.Precision.HIGHEST, preferred_element_t...  12.1 us
    ppermute x3, starting transfers between devices, with_halo(): lax.ppermute(lax.slice_in_dim(block, block.shape[dim] - width, None, axis...  11.1 us
    reshape x1, local copies, waits for them, and re-layouts, local(): flat = piece.reshape(number, -1)  10.6 us
    psum x1, blocking collectives, scales(): lax.psum((jnp.sum(own_drift * own_drift, axis=(1, 2, 3, 4)), jnp.sum(tang...  10 us
    add x16, other arithmetic, drift(): mobile = 0.5 + 1.0 / (1.0 + phi * phi)  8.8 us
  transfers between devices with their start and end apart: 7, of which 5 were waited for; matrix products, arithmetic and copies ran while one was open for 9% of the time, Pallas kernels for 0%

commit v1 on v0

v1 whole, which is shorter than its diff:
```python
import functools

import jax
import jax.numpy as jnp
from jax import lax
from jax.experimental import pallas as pl
from jax.experimental.pallas import tpu as pltpu
from jax.sharding import PartitionSpec as P

MESH = pl.DeviceIdType.MESH
WLEVELS = 16
KAPPA = 0.25
COUPLE = 0.3
STEP_SIZE = 0.004
EPSILON = 1e-06
SLOTS = 2
HALO = 4
RIM = 2


def kernel(
    n, m, per, depth, gx, chunks,
    state, sources, levels, out,
    land, edge, cells, mu_s, hm_s, b_s, t_s, sec_s, r_s, q_s, upd, sums, outbuf,
    pick, where_from, sbuf, *rest,
):
    rbufs = rest[:chunks]
    load_sem, out_sem, hs_sem, hr_sem, ss_sem, sr_sem, as_sem, ar_sem = rest[chunks:]
    me = lax.axis_index("img")
    slab = lax.axis_index("slab")
    entries = per * 2
    images = per * n
    planes = depth + 2 * HALO
    rows = gx * per
    own = depth * gx
    step = depth // chunks
    crow = step * gx

    def rem(a, b):
        return lax.rem(a, jnp.int32(b))

    nxt, prv = rem(me + 1, n), rem(me + n - 1, n)
    has_low, has_high = slab > 0, slab < m - 1

    def loads():
        return pltpu.make_async_copy(
            state, land.at[:, :, pl.ds(HALO * gx, own), :], load_sem
        )

    loads().start()

    barrier = pltpu.get_barrier_semaphore()

    def greet(i, s):
        pl.semaphore_signal(
            barrier, inc=1, device_id={"img": i, "slab": s}, device_id_type=MESH
        )

    for o in range(1, n):
        greet(rem(me + o, n), slab)
    for o in range(1, m):
        greet(me, rem(slab + o, m))

    @pl.when(has_low)
    def _():
        greet(nxt, slab - 1)
        greet(prv, slab - 1)

    @pl.when(has_high)
    def _():
        greet(nxt, slab + 1)
        greet(prv, slab + 1)

    count = (n - 1) + (m - 1) + jnp.where(has_low, 2, 0) + jnp.where(has_high, 2, 0)
    pl.semaphore_wait(barrier, count)

    def halo(k, src, dst, i, s):
        return pltpu.make_async_remote_copy(
            src_ref=src, dst_ref=dst, send_sem=hs_sem.at[k], recv_sem=hr_sem.at[k],
            device_id={"img": i, "slab": s}, device_id_type=MESH,
        )

    hr, rr, top = HALO * gx, RIM * gx, (HALO + depth) * gx
    last = per - 1
    to_high = [
        halo(0, state.at[:, :, pl.ds(own - hr, hr), :], land.at[:, :, pl.ds(0, hr), :], me, slab + 1),
        halo(4, state.at[last, :, pl.ds(own - rr, rr), :], edge.at[0, :, pl.ds(hr - rr, rr), :], nxt, slab + 1),
        halo(5, state.at[0, :, pl.ds(own - rr, rr), :], edge.at[1, :, pl.ds(hr - rr, rr), :], prv, slab + 1),
    ]
    to_low = [
        halo(1, state.at[:, :, pl.ds(0, hr), :], land.at[:, :, pl.ds(top, hr), :], me, slab - 1),
        halo(6, state.at[last, :, pl.ds(0, rr), :], edge.at[0, :, pl.ds(top, rr), :], nxt, slab - 1),
        halo(7, state.at[0, :, pl.ds(0, rr), :], edge.at[1, :, pl.ds(top, rr), :], prv, slab - 1),
    ]
    beside = [
        halo(2, state.at[last], edge.at[0, :, pl.ds(hr, own), :], nxt, slab),
        halo(3, state.at[0], edge.at[1, :, pl.ds(hr, own), :], prv, slab),
    ]

    @pl.when(has_high)
    def _():
        for c in to_high:
            c.start()

    @pl.when(has_low)
    def _():
        for c in to_low:
            c.start()

    for c in beside:
        c.start()

    def choose(d, carry):
        seen = jnp.int32(0)
        first = jnp.int32(0)
        second = jnp.int32(0)
        for e in range(entries):
            src = sources[d * per + e // 2, e % 2]
            mine = lax.div(src, jnp.int32(per)) == me
            place = lax.rem(src, jnp.int32(per))
            first = jnp.where(mine & (seen == 0), place, first)
            second = jnp.where(mine & (seen == 1), place, second)
            seen = seen + jnp.where(mine, 1, 0)
        pick[SLOTS * d] = first
        pick[SLOTS * d + 1] = second
        return carry

    lax.fori_loop(0, n, choose, 0)
    owners = []
    for e in range(entries):
        owner = lax.div(sources[me * per + e // 2, e % 2], jnp.int32(per))
        slot = jnp.int32(0)
        for before in owners:
            slot = jnp.where(before == owner, 1, slot)
        owners.append(owner)
        where_from[e] = SLOTS * owner + slot

    def rx(a, up):
        k = per if up else rows - per
        return jnp.concatenate([a[k:], a[:k]], axis=0)

    def ry(a, up):
        return pltpu.roll(a, a.shape[1] - 1 if up else 1, 1)

    def at(f, z):
        return pl.ds(pl.multiple_of((f * planes + z) * rows, 8), rows)

    def settle(lo, hi):
        def body(g, carry):
            for f in range(2):
                for i in range(per):
                    cells[pl.ds((f * planes + 2 * g) * rows + i, 8, stride=per), :] = land[
                        i, f, pl.ds(pl.multiple_of(8 * g, 8), 8), :
                    ]
            return carry

        lax.fori_loop(lo // 2, hi // 2, body, 0)

    def potentials(lo, hi):
        def body(z, carry):
            s = [cells[at(f, z), :] for f in range(2)]
            for f in range(2):
                a = s[f]
                sq = a * a
                near = cells[at(f, z + 1), :] + cells[at(f, z - 1), :]
                near = near + (rx(a, True) + rx(a, False)) + (ry(a, True) + ry(a, False))
                mu_s[at(f, z), :] = a * (sq + (6.0 * KAPPA - 1.0)) + COUPLE * s[1 - f] - KAPPA * near
                hm_s[at(f, z), :] = 0.25 + 0.5 / (1.0 + sq)
            return carry

        lax.fori_loop(lo, hi, body, 0)

    zero = jnp.zeros((rows, 128), jnp.float32)
    loads().wait()
    settle(HALO, HALO + depth)
    potentials(HALO + 1, HALO + depth - 1)

    @pl.when(has_low)
    def _():
        for k in range(3):
            halo(0, *((land.at[:, :, pl.ds(0, hr), :],) * 2), me, slab - 1).wait_recv() if k == 0 else \
                halo(3 + k, *((edge.at[k - 1, :, pl.ds(hr - rr, rr), :],) * 2), me, slab - 1).wait_recv()
        settle(0, HALO)

    @pl.when(has_high)
    def _():
        for k in range(3):
            halo(1, *((land.at[:, :, pl.ds(top, hr), :],) * 2), me, slab + 1).wait_recv() if k == 0 else \
                halo(5 + k, *((edge.at[k - 1, :, pl.ds(top, rr), :],) * 2), me, slab + 1).wait_recv()
        settle(HALO + depth, planes)

    @pl.when(jnp.logical_not(has_low))
    def _():
        for f in range(2):
            for z in range(HALO):
                cells[at(f, z), :] = zero
            for k in range(2):
                edge[k, f, pl.ds(hr - rr, rr), :] = zero[:rr]

    @pl.when(jnp.logical_not(has_high))
    def _():
        for f in range(2):
            for z in range(HALO + depth, planes):
                cells[at(f, z), :] = zero
            for k in range(2):
                edge[k, f, pl.ds(top, rr), :] = zero[:rr]

    potentials(1, HALO + 1)
    potentials(HALO + depth - 1, planes - 1)

    def mirror(ref):
        @pl.when(jnp.logical_not(has_low))
        def _():
            for f in range(2):
                ref[at(f, HALO - 1), :] = ref[at(f, HALO), :]

        @pl.when(jnp.logical_not(has_high))
        def _():
            for f in range(2):
                ref[at(f, HALO + depth), :] = ref[at(f, HALO + depth - 1), :]

    mirror(mu_s)
    for c in beside:
        c.wait_recv()

    line = lax.broadcasted_iota(jnp.int32, (per, 128), 0)
    at_last = line == per - 1
    at_first = line == 0

    def shifted(a, f, z):
        low, high = [], []
        for x in range(gx):
            tile = a[x * per : (x + 1) * per]
            r = pl.ds(z * gx + x, 1)
            before = jnp.broadcast_to(edge[0, f, r, :], (per, 128))
            after = jnp.broadcast_to(edge[1, f, r, :], (per, 128))
            low.append(pltpu.roll(jnp.where(at_last, before, tile), 1, 0))
            high.append(pltpu.roll(jnp.where(at_first, after, tile), per - 1, 0))
        return jnp.concatenate(low, axis=0), jnp.concatenate(high, axis=0)

    def fold(a):
        total = a[:per]
        for x in range(1, gx):
            total = total + a[x * per : (x + 1) * per]
        return total

    def z_flux(f, z):
        return (hm_s[at(f, z), :] + hm_s[at(f, z + 1), :]) * (mu_s[at(f, z + 1), :] - mu_s[at(f, z), :])

    def drifts(z, carry, summed):
        flux, acc_b, acc_t = list(carry[0:2]), carry[2], carry[3]
        for f in range(2):
            hm, mu = hm_s[at(f, z), :], mu_s[at(f, z), :]
            fz = (hm + hm_s[at(f, z + 1), :]) * (mu_s[at(f, z + 1), :] - mu)
            fx = (hm + rx(hm, True)) * (rx(mu, True) - mu)
            fy = (hm + ry(hm, True)) * (ry(mu, True) - mu)
            b = (fz - flux[f]) + (fx - rx(fx, False)) + (fy - ry(fy, False))
            flux[f] = fz
            a = cells[at(f, z), :]
            low, high = shifted(a, f, z)
            t = (high - low) * ((images - 1) / 2.0)
            b_s[at(f, z), :] = b
            t_s[at(f, z), :] = t
            sec_s[at(f, z), :] = (high + low - 2.0 * a) * float((images - 1) ** 2)
            if summed:
                acc_b = acc_b + fold(b * b)
                acc_t = acc_t + fold(t * t)
        return (flux[0], flux[1], acc_b, acc_t)

    none = jnp.zeros((per, 128), jnp.float32)
    carry = (z_flux(0, HALO - RIM - 1), z_flux(1, HALO - RIM - 1), none, none)
    carry = lax.fori_loop(HALO - RIM, HALO, lambda z, c: drifts(z, c, False), carry)
    carry = lax.fori_loop(HALO, HALO + depth, lambda z, c: drifts(z, c, True), carry)
    carry = lax.fori_loop(HALO + depth, HALO + depth + RIM, lambda z, c: drifts(z, c, False), carry)
    sums[0, 0] = carry[2]
    sums[0, 1] = carry[3]

    def share(o):
        return pltpu.make_async_remote_copy(
            src_ref=sums.at[0], dst_ref=sums.at[o], send_sem=ss_sem.at[o], recv_sem=sr_sem.at[o],
            device_id={"img": me, "slab": rem(slab + o, m)}, device_id_type=MESH,
        )

    for o in range(1, m):
        share(o).start()
    for o in range(1, m):
        share(o).wait_recv()
    total_b, total_t = sums[0, 0], sums[0, 1]
    for o in range(1, m):
        total_b = total_b + sums[o, 0]
        total_t = total_t + sums[o, 1]
    total_b = jnp.sum(total_b, axis=1, keepdims=True)
    total_t = jnp.sum(total_t, axis=1, keepdims=True)
    lam = jnp.sqrt(total_b) / jnp.sqrt(total_t + EPSILON)
    lam = jnp.broadcast_to(lam, (per, 128))
    ids = line + me * per
    inner = jnp.where((ids > 0) & (ids < images - 1), STEP_SIZE, 0.0).astype(jnp.float32)

    def wide(a):
        return jnp.concatenate([a] * gx, axis=0)

    lam_w, inner_w = wide(lam), wide(inner)
    square_w = wide(inner * lam * lam)

    def moments(z, carry):
        for f in range(2):
            t_s[at(f, z), :] = lam_w * t_s[at(f, z), :] - b_s[at(f, z), :]
        return carry

    lax.fori_loop(HALO - RIM, HALO + depth + RIM, moments, 0)
    mirror(t_s)

    def adjoint(z, carry):
        flux, prod = list(carry[0:2]), list(carry[2:4])
        for f in range(2):
            hm, mu, mo = hm_s[at(f, z), :], mu_s[at(f, z), :], t_s[at(f, z), :]
            dz = t_s[at(f, z + 1), :] - mo
            dx = rx(mo, True) - mo
            dy = ry(mo, True) - mo
            fz = (hm + hm_s[at(f, z + 1), :]) * dz
            fx = (hm + rx(hm, True)) * dx
            fy = (hm + ry(hm, True)) * dy
            pz = (mu_s[at(f, z + 1), :] - mu) * dz
            px = (rx(mu, True) - mu) * dx
            py = (ry(mu, True) - mu) * dy
            r_s[at(f, z), :] = (fz - flux[f]) + (fx - rx(fx, False)) + (fy - ry(fy, False))
            q_s[at(f, z), :] = (pz + prod[f]) + (px + rx(px, False)) + (py + ry(py, False))
            flux[f], prod[f] = fz, pz
        return (flux[0], flux[1], prod[0], prod[1])

    def finish(z, carry):
        r = [r_s[at(f, z), :] for f in range(2)]
        for f in range(2):
            a, c = cells[at(f, z), :], r[f]
            near = r_s[at(f, z + 1), :] + r_s[at(f, z - 1), :]
            near = near + (rx(c, True) + rx(c, False)) + (ry(c, True) + ry(c, False))
            inv = 2.0 * hm_s[at(f, z), :] - 0.5
            pulled = (3.0 * (a * a) + (6.0 * KAPPA - 1.0)) * c + COUPLE * r[1 - f] - KAPPA * near
            pulled = pulled + (a * inv) * (inv * q_s[at(f, z), :])
            upd[at(f, z), :] = a + (square_w * sec_s[at(f, z), :] + inner_w * pulled)
        return carry

    def pack(dest, c, put):
        for s in range(SLOTS):
            image = pick[SLOTS * dest + s]
            for f in range(2):
                for g in range(crow // 8):
                    start = (f * planes + HALO + c * step) * rows + g * 8 * per
                    put(s, f, pl.ds(8 * g, 8), upd[pl.ds(start + image, 8, stride=per), :])

    def send(c, o):
        return pltpu.make_async_remote_copy(
            src_ref=sbuf.at[c, o - 1], dst_ref=rbufs[c].at[pl.ds(SLOTS * me, SLOTS)],
            send_sem=as_sem.at[c, o], recv_sem=ar_sem.at[c, o],
            device_id={"img": rem(me + o, n), "slab": slab}, device_id_type=MESH,
        )

    def arrival(c, o):
        src = rem(me + n - o, n)
        return pltpu.make_async_remote_copy(
            src_ref=sbuf.at[c, o - 1], dst_ref=rbufs[c].at[pl.ds(SLOTS * src, SLOTS)],
            send_sem=as_sem.at[c, o], recv_sem=ar_sem.at[c, o],
            device_id={"img": src, "slab": slab}, device_id_type=MESH,
        )

    first = HALO - 2
    carry = []
    for f in range(2):
        dz = t_s[at(f, first + 1), :] - t_s[at(f, first), :]
        carry.append((hm_s[at(f, first), :] + hm_s[at(f, first + 1), :]) * dz)
    for f in range(2):
        dz = t_s[at(f, first + 1), :] - t_s[at(f, first), :]
        carry.append((mu_s[at(f, first + 1), :] - mu_s[at(f, first), :]) * dz)
    carry = tuple(carry)
    lo = HALO - 1
    for c in range(chunks):
        hi = HALO + (c + 1) * step + 1
        carry = lax.fori_loop(lo, hi, adjoint, carry)
        lo = hi
        if c == 0:
            @pl.when(jnp.logical_not(has_low))
            def _():
                for f in range(2):
                    r_s[at(f, HALO - 1), :] = zero
        if c == chunks - 1:
            @pl.when(jnp.logical_not(has_high))
            def _():
                for f in range(2):
                    r_s[at(f, HALO + depth), :] = zero
        lax.fori_loop(HALO + c * step, HALO + (c + 1) * step, finish, 0)
        for o in range(1, n):
            def put(s, f, where, value):
                sbuf[c, o - 1, s, f, where, :] = value

            pack(rem(me + o, n), c, put)
            send(c, o).start()

        def keep(s, f, where, value):
            rbufs[c][SLOTS * me + s, f, where, :] = value

        pack(me, c, keep)

    def store(c):
        return pltpu.make_async_copy(
            outbuf.at[:, :, pl.ds(c * crow, crow), :], out.at[:, :, pl.ds(c * crow, crow), :], out_sem.at[c]
        )

    for c in range(chunks):
        for o in range(1, n):
            arrival(c, o).wait_recv()
        for j in range(per):
            weight = (levels[j].astype(jnp.float32) + 1.0) * (1.0 / (WLEVELS + 1.0))
            one, two = where_from[2 * j], where_from[2 * j + 1]
            for f in range(2):
                outbuf[j, f, pl.ds(c * crow, crow), :] = (
                    weight * rbufs[c][one, f] + (1.0 - weight) * rbufs[c][two, f]
                )
        store(c).start()

    for c in range(chunks):
        for o in range(1, n):
            send(c, o).wait_send()
    for o in range(1, m):
        share(o).wait_send()
    for c in beside:
        c.wait_send()

    @pl.when(has_high)
    def _():
        for c in to_high:
            c.wait_send()

    @pl.when(has_low)
    def _():
        for c in to_low:
            c.wait_send()

    for c in range(chunks):
        store(c).wait()


def local(n, m, state, sources, levels):
    per, _, depth, gx, gy = state.shape
    planes = depth + 2 * HALO
    chunks = 4
    crow = depth // chunks * gx
    field = pltpu.VMEM((2 * planes * gx * per, gy), jnp.float32)
    flat = state.reshape(per, 2, depth * gx, gy)
    moved = pl.pallas_call(
        functools.partial(kernel, n, m, per, depth, gx, chunks),
        out_shape=jax.ShapeDtypeStruct(flat.shape, jnp.float32),
        in_specs=[
            pl.BlockSpec(memory_space=pl.ANY),
            pl.BlockSpec(memory_space=pltpu.SMEM),
            pl.BlockSpec(memory_space=pltpu.SMEM),
        ],
        out_specs=pl.BlockSpec(memory_space=pl.ANY),
        scratch_shapes=[
            pltpu.VMEM((per, 2, planes * gx, gy), jnp.float32),
            pltpu.VMEM((2, 2, planes * gx, gy), jnp.float32),
        ]
        + [field] * 9
        + [
            pltpu.VMEM((m, 2, per, gy), jnp.float32),
            pltpu.VMEM((per, 2, depth * gx, gy), jnp.float32),
            pltpu.SMEM((SLOTS * n,), jnp.int32),
            pltpu.SMEM((2 * per,), jnp.int32),
            pltpu.VMEM((chunks, n - 1, SLOTS, 2, crow, gy), jnp.float32),
        ]
        + [pltpu.VMEM((SLOTS * n, 2, crow, gy), jnp.float32)] * chunks
        + [
            pltpu.SemaphoreType.DMA,
            pltpu.SemaphoreType.DMA((chunks,)),
            pltpu.SemaphoreType.DMA((8,)),
            pltpu.SemaphoreType.DMA((8,)),
            pltpu.SemaphoreType.DMA((m,)),
            pltpu.SemaphoreType.DMA((m,)),
            pltpu.SemaphoreType.DMA((chunks, n)),
            pltpu.SemaphoreType.DMA((chunks, n)),
        ],
        compiler_params=pltpu.CompilerParams(
            collective_id=0, has_side_effects=True, vmem_limit_bytes=48 * 1024 * 1024
        ),
        cost_estimate=pl.CostEstimate(
            flops=110 * flat.size, bytes_accessed=8 * flat.size, transcendentals=flat.size
        ),
    )(flat, sources, levels)
    return moved.reshape(state.shape)


def solution(mesh):
    return jax.shard_map(
        functools.partial(local, mesh.shape["img"], mesh.shape["slab"]),
        mesh=mesh,
        in_specs=(P("img", None, "slab", None, None), P(), P("img")),
        out_specs=P("img", None, "slab", None, None),
        check_vma=False,
    )
```

time: 225 us -> 53.3 us (0.24)
  local copies, waits for them, and re-layouts: 68.2 us -> 3.53 us
  waiting for transfers between devices: 62.7 us -> 0 us
  Pallas kernels: 0 us -> 49.3 us
  other arithmetic: 39.7 us -> 0 us
  starting transfers between devices: 14.9 us -> 0 us
  between operations: 13.6 us -> 0.01 us
  matrix products: 12.3 us -> 0 us
  blocking collectives: 10 us -> 0 us
  loops' own time: 2.63 us -> 0 us
    all_gather x1 -> x0, waiting for transfers between devices: 52.4 us -> none  [local(): piece = lax.all_gather(updated, 'img', axis=0, tiled=True)]
    pallas_call x0 -> x1, Pallas kernels: none -> 49.3 us  [local(): pl.pallas_call(functools.partial(kernel, n, m, per, depth, gx, chunks), o...]
    slice x179 -> x0, local copies, waits for them, and re-layouts: 16.4 us -> none  [the longest x32 4.89 us: drift(): lapl = lapl + jnp.roll(phi, 1, 3) + jnp.roll(phi, -1, 3) - 6.0 * phi]
    ppermute x6 -> x0, starting transfers between devices: 14.9 us -> none  [the longest x3 11.1 us: with_halo(): lax.ppermute(lax.slice_in_dim(block, block.shape[dim] - width, None, axis...]
    all_gather x1 -> x0, local copies, waits for them, and re-layouts: 14.9 us -> none  [local(): piece = lax.all_gather(updated, 'img', axis=0, tiled=True)]
    dot_general x1 -> x0, matrix products: 12.3 us -> none  [local(): jnp.dot(table, flat, precision=lax.Precision.HIGHEST, preferred_element_t...]
    dot_general x2 -> x0, local copies, waits for them, and re-layouts: 12.1 us -> none  [local(): jnp.dot(table, flat, precision=lax.Precision.HIGHEST, preferred_element_t...]
    reshape x1 -> x0, local copies, waits for them, and re-layouts: 10.6 us -> none  [local(): flat = piece.reshape(number, -1)]
  transfers between devices with their start and end apart: 7 -> 0, of which waited for: 5 -> 0; matrix products, arithmetic and copies ran while one was open for 9% -> 0% of each run, Pallas kernels for 0% -> 0%
where the time goes in v1:
time: 53.3 us; the launch traced here: 52.8 us
  Pallas kernels  49.3 us (92%)
  local copies, waits for them, and re-layouts  3.53 us (7%)
    pallas_call x1, Pallas kernels, local(): pl.pallas_call(functools.partial(kernel, n, m, per, depth, gx, chunks), o...  49.3 us
    unnamed x8, local copies, waits for them, and re-layouts  3.53 us

profile of v1, /device:TPU:0, one launch (start us, length us, event | category | flops | bytes accessed | tf_op | source)
XLA Modules:
  0.0 52.8 jit_solution(14733453792957966544)
XLA Ops:
  0.0 0.0 copy-start.2
  0.0 0.7 %copy-done.2 = s32[64,2]{0,1:T(2,128)S(1)} copy-done((s32[64,2]{0,1:T(2,128)S(1)}, s32[64,2]{0,1:T(2,128)}, u32[]{:S(2)}) %copy-start.2) | copy-done | bytes 536
  0.7 0.0 copy-start.1
  0.7 0.1 copy.4.sources
  0.8 0.6 %copy-done.1 = s32[8]{0:T(128)S(1)} copy-done((s32[8]{0:T(128)S(1)}, s32[8]{0:T(128)}, u32[]{:S(2)}) %copy-start.1) | copy-done | bytes 56
  1.3 0.0 copy-start
  1.3 1.2 %copy-done = f32[8,2,32,4,128]{4,3,2,1,0:T(4,128)S(1)} copy-done((f32[8,2,32,4,128]{4,3,2,1,0:T(4,128)S(1)}, f32[8,2,32,4,128]{4,3,2,1,0:T(4,128)}, u32[]{:S(2)}) %copy-start) | copy-done | bytes 1048600
  2.6 49.3 %shard_map.37 = f32[8,2,128,128]{3,2,1,0:T(8,128)S(1)} custom-call(f32[8,2,128,128]{3,2,1,0:T(8,128)S(1)} %bitcast.3, s32[64,2]{1,0:T(8,128)S(1)} %copy.4.sources, s32[8]{0:T(128)S(1)} %copy-done.1), custom_call_target="tpu_custom_call" | custom-call | flops 28835840 | bytes 2097152 | tf_op jit(solution)/shard_map/pallas_call | solution.py:449
  51.9 1.0 %copy.6 = f32[8,2,32,4,128]{4,3,2,1,0:T(4,128)} copy(f32[8,2,32,4,128]{4,3,2,1,0:T(4,128)S(1)} %bitcast.2) | data formatting | bytes 2097152
Async XLA Ops:
  0.0 0.7 %copy-start.2 = (s32[64,2]{0,1:T(2,128)S(1)}, s32[64,2]{0,1:T(2,128)}, u32[]{:S(2)}) copy-start(s32[64,2]{0,1:T(2,128)} %param.4) | copy-start | bytes 1540
  0.7 0.7 %copy-start.1 = (s32[8]{0:T(128)S(1)}, s32[8]{0:T(128)}, u32[]{:S(2)}) copy-start(s32[8]{0:T(128)} %levels.1) | copy-start | bytes 100
  1.3 1.2 %copy-start = (f32[8,2,32,4,128]{4,3,2,1,0:T(4,128)S(1)}, f32[8,2,32,4,128]{4,3,2,1,0:T(4,128)}, u32[]{:S(2)}) copy-start(f32[8,2,32,4,128]{4,3,2,1,0:T(4,128)} %param.3) | copy-start | bytes 3145732

commit v2 on v1

--- a/solution.py
+++ b/solution.py
@@ -19,13 +19,15 @@
 
 
 def kernel(
-    n, m, per, depth, gx, chunks,
-    state, sources, levels, out,
-    land, edge, cells, mu_s, hm_s, b_s, t_s, sec_s, r_s, q_s, upd, sums, outbuf,
+    n, m, per, depth, gx, sizes,
+    state, sources_hbm, levels_hbm, out,
+    sources, levels, land, edge, cells, mu_s, hm_s, b_s, t_s, sec_s, r_s, q_s, upd, sums, outbuf,
     pick, where_from, sbuf, *rest,
 ):
-    rbufs = rest[:chunks]
-    load_sem, out_sem, hs_sem, hr_sem, ss_sem, sr_sem, as_sem, ar_sem = rest[chunks:]
+    chunks = len(sizes)
+    starts = [sum(sizes[:c]) for c in range(chunks)]
+    sbufs, rbufs = (sbuf,) + rest[: chunks - 1], rest[chunks - 1 : 2 * chunks - 1]
+    load_sem, out_sem, hs_sem, hr_sem, ss_sem, sr_sem, as_sem, ar_sem = rest[2 * chunks - 1 :]
     me = lax.axis_index("img")
     slab = lax.axis_index("slab")
     entries = per * 2
@@ -33,21 +35,35 @@
     planes = depth + 2 * HALO
     rows = gx * per
     own = depth * gx
-    step = depth // chunks
-    crow = step * gx
 
     def rem(a, b):
         return lax.rem(a, jnp.int32(b))
 
     nxt, prv = rem(me + 1, n), rem(me + n - 1, n)
+
+    def partner(o):
+        other, bit = me, 1
+        while bit < n:
+            if o & bit:
+                other = other + bit - 2 * bit * rem(lax.div(me, jnp.int32(bit)), 2)
+            bit *= 2
+        return other
+
+    order = sorted(range(1, n), key=lambda o: (o < 2, o % 2, -(o // 2)))
     has_low, has_high = slab > 0, slab < m - 1
 
     def loads():
         return pltpu.make_async_copy(
-            state, land.at[:, :, pl.ds(HALO * gx, own), :], load_sem
+            state, land.at[:, :, pl.ds(HALO * gx, own), :], load_sem.at[0]
         )
 
+    tables = [
+        pltpu.make_async_copy(sources_hbm, sources, load_sem.at[1]),
+        pltpu.make_async_copy(levels_hbm, levels, load_sem.at[2]),
+    ]
     loads().start()
+    for c in tables:
+        c.start()
 
     barrier = pltpu.get_barrier_semaphore()
 
@@ -57,7 +73,7 @@
         )
 
     for o in range(1, n):
-        greet(rem(me + o, n), slab)
+        greet(partner(o), slab)
     for o in range(1, m):
         greet(me, rem(slab + o, m))
 
@@ -115,7 +131,7 @@
         first = jnp.int32(0)
         second = jnp.int32(0)
         for e in range(entries):
-            src = sources[d * per + e // 2, e % 2]
+            src = sources[e % 2, d * per + e // 2]
             mine = lax.div(src, jnp.int32(per)) == me
             place = lax.rem(src, jnp.int32(per))
             first = jnp.where(mine & (seen == 0), place, first)
@@ -125,10 +141,12 @@
         pick[SLOTS * d + 1] = second
         return carry
 
+    for c in tables:
+        c.wait()
     lax.fori_loop(0, n, choose, 0)
     owners = []
     for e in range(entries):
-        owner = lax.div(sources[me * per + e // 2, e % 2], jnp.int32(per))
+        owner = lax.div(sources[e % 2, me * per + e // 2], jnp.int32(per))
         slot = jnp.int32(0)
         for before in owners:
             slot = jnp.where(before == owner, 1, slot)
@@ -143,7 +161,24 @@
         return pltpu.roll(a, a.shape[1] - 1 if up else 1, 1)
 
     def at(f, z):
-        return pl.ds(pl.multiple_of((f * planes + z) * rows, 8), rows)
+        start = (f * planes + z) * rows
+        return pl.ds(start if isinstance(start, int) else pl.multiple_of(start, 8), rows)
+
+    def loop(lo, hi, body, carry, k=2):
+        full = (hi - lo) // k
+        if full:
+            carry = lax.fori_loop(0, full, lambda i, c: body(lo + i * k, c, k), carry)
+        if lo + full * k < hi:
+            carry = body(lo + full * k, carry, hi - lo - full * k)
+        return carry
+
+    def take(ref, z, j0, j1):
+        return [{j: ref[at(f, z + j), :] for j in range(j0, j1)} for f in range(2)]
+
+    def give(ref, z, values):
+        for f in range(2):
+            for j, v in values[f].items():
+                ref[at(f, z + j), :] = v
 
     def settle(lo, hi):
         def body(g, carry):
@@ -157,18 +192,22 @@
         lax.fori_loop(lo // 2, hi // 2, body, 0)
 
     def potentials(lo, hi):
-        def body(z, carry):
-            s = [cells[at(f, z), :] for f in range(2)]
-            for f in range(2):
-                a = s[f]
-                sq = a * a
-                near = cells[at(f, z + 1), :] + cells[at(f, z - 1), :]
-                near = near + (rx(a, True) + rx(a, False)) + (ry(a, True) + ry(a, False))
-                mu_s[at(f, z), :] = a * (sq + (6.0 * KAPPA - 1.0)) + COUPLE * s[1 - f] - KAPPA * near
-                hm_s[at(f, z), :] = 0.25 + 0.5 / (1.0 + sq)
+        def body(z, carry, k):
+            s = take(cells, z, -1, k + 1)
+            mu, hm = [{}, {}], [{}, {}]
+            for j in range(k):
+                for f in range(2):
+                    a = s[f][j]
+                    sq = a * a
+                    near = (s[f][j + 1] + s[f][j - 1]) + (rx(a, True) + rx(a, False))
+                    near = near + (ry(a, True) + ry(a, False))
+                    mu[f][j] = a * (sq + (6.0 * KAPPA - 1.0)) + COUPLE * s[1 - f][j] - KAPPA * near
+                    hm[f][j] = 0.25 + 0.5 / (1.0 + sq)
+            give(mu_s, z, mu)
+            give(hm_s, z, hm)
             return carry
 
-        lax.fori_loop(lo, hi, body, 0)
+        loop(lo, hi, body, 0)
 
     zero = jnp.zeros((rows, 128), jnp.float32)
     loads().wait()
@@ -247,31 +286,36 @@
     def z_flux(f, z):
         return (hm_s[at(f, z), :] + hm_s[at(f, z + 1), :]) * (mu_s[at(f, z + 1), :] - mu_s[at(f, z), :])
 
-    def drifts(z, carry, summed):
+    def drifts(summed, z, carry, k):
         flux, acc_b, acc_t = list(carry[0:2]), carry[2], carry[3]
-        for f in range(2):
-            hm, mu = hm_s[at(f, z), :], mu_s[at(f, z), :]
-            fz = (hm + hm_s[at(f, z + 1), :]) * (mu_s[at(f, z + 1), :] - mu)
-            fx = (hm + rx(hm, True)) * (rx(mu, True) - mu)
-            fy = (hm + ry(hm, True)) * (ry(mu, True) - mu)
-            b = (fz - flux[f]) + (fx - rx(fx, False)) + (fy - ry(fy, False))
-            flux[f] = fz
-            a = cells[at(f, z), :]
-            low, high = shifted(a, f, z)
-            t = (high - low) * ((images - 1) / 2.0)
-            b_s[at(f, z), :] = b
-            t_s[at(f, z), :] = t
-            sec_s[at(f, z), :] = (high + low - 2.0 * a) * float((images - 1) ** 2)
-            if summed:
-                acc_b = acc_b + fold(b * b)
-                acc_t = acc_t + fold(t * t)
+        hm, mu, s = take(hm_s, z, 0, k + 1), take(mu_s, z, 0, k + 1), take(cells, z, 0, k)
+        near = [[shifted(s[f][j], f, z + j) for j in range(k)] for f in range(2)]
+        b, t, sec = [{}, {}], [{}, {}], [{}, {}]
+        for j in range(k):
+            for f in range(2):
+                h, u = hm[f][j], mu[f][j]
+                fz = (h + hm[f][j + 1]) * (mu[f][j + 1] - u)
+                fx = (h + rx(h, True)) * (rx(u, True) - u)
+                fy = (h + ry(h, True)) * (ry(u, True) - u)
+                b[f][j] = (fz - flux[f]) + (fx - rx(fx, False)) + (fy - ry(fy, False))
+                flux[f] = fz
+                low, high = near[f][j]
+                t[f][j] = (high - low) * ((images - 1) / 2.0)
+                sec[f][j] = (high + low - 2.0 * s[f][j]) * float((images - 1) ** 2)
+                if summed:
+                    acc_b = acc_b + fold(b[f][j] * b[f][j])
+                    acc_t = acc_t + fold(t[f][j] * t[f][j])
+        give(b_s, z, b)
+        give(t_s, z, t)
+        give(sec_s, z, sec)
         return (flux[0], flux[1], acc_b, acc_t)
 
     none = jnp.zeros((per, 128), jnp.float32)
     carry = (z_flux(0, HALO - RIM - 1), z_flux(1, HALO - RIM - 1), none, none)
-    carry = lax.fori_loop(HALO - RIM, HALO, lambda z, c: drifts(z, c, False), carry)
-    carry = lax.fori_loop(HALO, HALO + depth, lambda z, c: drifts(z, c, True), carry)
-    carry = lax.fori_loop(HALO + depth, HALO + depth + RIM, lambda z, c: drifts(z, c, False), carry)
+    plain, summing = functools.partial(drifts, False), functools.partial(drifts, True)
+    carry = loop(HALO - RIM, HALO, plain, carry)
+    carry = loop(HALO, HALO + depth, summing, carry)
+    carry = loop(HALO + depth, HALO + depth + RIM, plain, carry)
     sums[0, 0] = carry[2]
     sums[0, 1] = carry[3]
 
@@ -283,6 +327,8 @@
 
     for o in range(1, m):
         share(o).start()
+    mirror(t_s)
+    mirror(b_s)
     for o in range(1, m):
         share(o).wait_recv()
     total_b, total_t = sums[0, 0], sums[0, 1]
@@ -302,80 +348,78 @@
     lam_w, inner_w = wide(lam), wide(inner)
     square_w = wide(inner * lam * lam)
 
-    def moments(z, carry):
-        for f in range(2):
-            t_s[at(f, z), :] = lam_w * t_s[at(f, z), :] - b_s[at(f, z), :]
-        return carry
-
-    lax.fori_loop(HALO - RIM, HALO + depth + RIM, moments, 0)
-    mirror(t_s)
-
-    def adjoint(z, carry):
+    def moment(f, z):
+        return lam_w * t_s[at(f, z), :] - b_s[at(f, z), :]
+
+    def adjoint(z, carry, k):
         flux, prod = list(carry[0:2]), list(carry[2:4])
-        for f in range(2):
-            hm, mu, mo = hm_s[at(f, z), :], mu_s[at(f, z), :], t_s[at(f, z), :]
-            dz = t_s[at(f, z + 1), :] - mo
-            dx = rx(mo, True) - mo
-            dy = ry(mo, True) - mo
-            fz = (hm + hm_s[at(f, z + 1), :]) * dz
-            fx = (hm + rx(hm, True)) * dx
-            fy = (hm + ry(hm, True)) * dy
-            pz = (mu_s[at(f, z + 1), :] - mu) * dz
-            px = (rx(mu, True) - mu) * dx
-            py = (ry(mu, True) - mu) * dy
-            r_s[at(f, z), :] = (fz - flux[f]) + (fx - rx(fx, False)) + (fy - ry(fy, False))
-            q_s[at(f, z), :] = (pz + prod[f]) + (px + rx(px, False)) + (py + ry(py, False))
-            flux[f], prod[f] = fz, pz
+        hm, mu = take(hm_s, z, 0, k + 1), take(mu_s, z, 0, k + 1)
+        mo = [{j: moment(f, z + j) for j in range(k + 1)} for f in range(2)]
+        r, q = [{}, {}], [{}, {}]
+        for j in range(k):
+            for f in range(2):
+                h, u, o = hm[f][j], mu[f][j], mo[f][j]
+                dz, dx, dy = mo[f][j + 1] - o, rx(o, True) - o, ry(o, True) - o
+                fz = (h + hm[f][j + 1]) * dz
+                fx = (h + rx(h, True)) * dx
+                fy = (h + ry(h, True)) * dy
+                pz = (mu[f][j + 1] - u) * dz
+                px = (rx(u, True) - u) * dx
+                py = (ry(u, True) - u) * dy
+                r[f][j] = (fz - flux[f]) + (fx - rx(fx, False)) + (fy - ry(fy, False))
+                q[f][j] = (pz + prod[f]) + (px + rx(px, False)) + (py + ry(py, False))
+                flux[f], prod[f] = fz, pz
+        give(r_s, z, r)
+        give(q_s, z, q)
         return (flux[0], flux[1], prod[0], prod[1])
 
-    def finish(z, carry):
-        r = [r_s[at(f, z), :] for f in range(2)]
-        for f in range(2):
-            a, c = cells[at(f, z), :], r[f]
-            near = r_s[at(f, z + 1), :] + r_s[at(f, z - 1), :]
-            near = near + (rx(c, True) + rx(c, False)) + (ry(c, True) + ry(c, False))
-            inv = 2.0 * hm_s[at(f, z), :] - 0.5
-            pulled = (3.0 * (a * a) + (6.0 * KAPPA - 1.0)) * c + COUPLE * r[1 - f] - KAPPA * near
-            pulled = pulled + (a * inv) * (inv * q_s[at(f, z), :])
-            upd[at(f, z), :] = a + (square_w * sec_s[at(f, z), :] + inner_w * pulled)
+    def finish(z, carry, k):
+        r, s, hm = take(r_s, z, -1, k + 1), take(cells, z, 0, k), take(hm_s, z, 0, k)
+        q, sec = take(q_s, z, 0, k), take(sec_s, z, 0, k)
+        new = [{}, {}]
+        for j in range(k):
+            for f in range(2):
+                a, c = s[f][j], r[f][j]
+                near = (r[f][j + 1] + r[f][j - 1]) + (rx(c, True) + rx(c, False))
+                near = near + (ry(c, True) + ry(c, False))
+                inv = 2.0 * hm[f][j] - 0.5
+                pulled = (3.0 * (a * a) + (6.0 * KAPPA - 1.0)) * c + COUPLE * r[1 - f][j] - KAPPA * near
+                pulled = pulled + (a * inv) * (inv * q[f][j])
+                new[f][j] = a + (square_w * sec[f][j] + inner_w * pulled)
+        give(upd, z, new)
         return carry
 
     def pack(dest, c, put):
         for s in range(SLOTS):
             image = pick[SLOTS * dest + s]
             for f in range(2):
-                for g in range(crow // 8):
-                    start = (f * planes + HALO + c * step) * rows + g * 8 * per
+                for g in range(sizes[c] * gx // 8):
+                    start = (f * planes + HALO + starts[c]) * rows + g * 8 * per
                     put(s, f, pl.ds(8 * g, 8), upd[pl.ds(start + image, 8, stride=per), :])
 
+    def exchange(c, o, to):
+        return pltpu.make_async_remote_copy(
+            src_ref=sbufs[c].at[o - 1], dst_ref=rbufs[c].at[pl.ds(SLOTS * to, SLOTS)],
+            send_sem=as_sem.at[c, o], recv_sem=ar_sem.at[c, o],
+            device_id={"img": partner(o), "slab": slab}, device_id_type=MESH,
+        )
+
     def send(c, o):
-        return pltpu.make_async_remote_copy(
-            src_ref=sbuf.at[c, o - 1], dst_ref=rbufs[c].at[pl.ds(SLOTS * me, SLOTS)],
-            send_sem=as_sem.at[c, o], recv_sem=ar_sem.at[c, o],
-            device_id={"img": rem(me + o, n), "slab": slab}, device_id_type=MESH,
-        )
+        return exchange(c, o, me)
 
     def arrival(c, o):
-        src = rem(me + n - o, n)
-        return pltpu.make_async_remote_copy(
-            src_ref=sbuf.at[c, o - 1], dst_ref=rbufs[c].at[pl.ds(SLOTS * src, SLOTS)],
-            send_sem=as_sem.at[c, o], recv_sem=ar_sem.at[c, o],
-            device_id={"img": src, "slab": slab}, device_id_type=MESH,
-        )
+        return exchange(c, o, partner(o))
 
     first = HALO - 2
-    carry = []
-    for f in range(2):
-        dz = t_s[at(f, first + 1), :] - t_s[at(f, first), :]
-        carry.append((hm_s[at(f, first), :] + hm_s[at(f, first + 1), :]) * dz)
-    for f in range(2):
-        dz = t_s[at(f, first + 1), :] - t_s[at(f, first), :]
-        carry.append((mu_s[at(f, first + 1), :] - mu_s[at(f, first), :]) * dz)
-    carry = tuple(carry)
+    dz = [moment(f, first + 1) - moment(f, first) for f in range(2)]
+    carry = tuple(
+        [(hm_s[at(f, first), :] + hm_s[at(f, first + 1), :]) * dz[f] for f in range(2)]
+        + [(mu_s[at(f, first + 1), :] - mu_s[at(f, first), :]) * dz[f] for f in range(2)]
+    )
     lo = HALO - 1
     for c in range(chunks):
-        hi = HALO + (c + 1) * step + 1
-        carry = lax.fori_loop(lo, hi, adjoint, carry)
+        hi = HALO + starts[c] + sizes[c] + 1
+        carry = loop(lo, hi, adjoint, carry)
         lo = hi
         if c == 0:
             @pl.when(jnp.logical_not(has_low))
@@ -387,12 +431,12 @@
             def _():
                 for f in range(2):
                     r_s[at(f, HALO + depth), :] = zero
-        lax.fori_loop(HALO + c * step, HALO + (c + 1) * step, finish, 0)
-        for o in range(1, n):
+        loop(HALO + starts[c], HALO + starts[c] + sizes[c], finish, 0)
+        for o in order:
             def put(s, f, where, value):
-                sbuf[c, o - 1, s, f, where, :] = value
-
-            pack(rem(me + o, n), c, put)
+                sbufs[c][o - 1, s, f, where, :] = value
+
+            pack(partner(o), c, put)
             send(c, o).start()
 
         def keep(s, f, where, value):
@@ -401,18 +445,17 @@
         pack(me, c, keep)
 
     def store(c):
-        return pltpu.make_async_copy(
-            outbuf.at[:, :, pl.ds(c * crow, crow), :], out.at[:, :, pl.ds(c * crow, crow), :], out_sem.at[c]
-        )
+        part = pl.ds(starts[c] * gx, sizes[c] * gx)
+        return pltpu.make_async_copy(outbuf.at[:, :, part, :], out.at[:, :, part, :], out_sem.at[c])
 
     for c in range(chunks):
-        for o in range(1, n):
+        for o in order:
             arrival(c, o).wait_recv()
         for j in range(per):
             weight = (levels[j].astype(jnp.float32) + 1.0) * (1.0 / (WLEVELS + 1.0))
             one, two = where_from[2 * j], where_from[2 * j + 1]
             for f in range(2):
-                outbuf[j, f, pl.ds(c * crow, crow), :] = (
+                outbuf[j, f, pl.ds(starts[c] * gx, sizes[c] * gx), :] = (
                     weight * rbufs[c][one, f] + (1.0 - weight) * rbufs[c][two, f]
                 )
         store(c).start()
@@ -442,20 +485,17 @@
 def local(n, m, state, sources, levels):
     per, _, depth, gx, gy = state.shape
     planes = depth + 2 * HALO
-    chunks = 4
-    crow = depth // chunks * gx
+    sizes = (4, 8, 8, 8, 4)
     field = pltpu.VMEM((2 * planes * gx * per, gy), jnp.float32)
     flat = state.reshape(per, 2, depth * gx, gy)
     moved = pl.pallas_call(
-        functools.partial(kernel, n, m, per, depth, gx, chunks),
+        functools.partial(kernel, n, m, per, depth, gx, sizes),
         out_shape=jax.ShapeDtypeStruct(flat.shape, jnp.float32),
-        in_specs=[
-            pl.BlockSpec(memory_space=pl.ANY),
-            pl.BlockSpec(memory_space=pltpu.SMEM),
-            pl.BlockSpec(memory_space=pltpu.SMEM),
-        ],
+        in_specs=[pl.BlockSpec(memory_space=pltpu.HBM)] * 3,
         out_specs=pl.BlockSpec(memory_space=pl.ANY),
         scratch_shapes=[
+            pltpu.SMEM((2, n * per), jnp.int32),
+            pltpu.SMEM((per,), jnp.int32),
             pltpu.VMEM((per, 2, planes * gx, gy), jnp.float32),
             pltpu.VMEM((2, 2, planes * gx, gy), jnp.float32),
         ]
@@ -465,26 +505,26 @@
             pltpu.VMEM((per, 2, depth * gx, gy), jnp.float32),
             pltpu.SMEM((SLOTS * n,), jnp.int32),
             pltpu.SMEM((2 * per,), jnp.int32),
-            pltpu.VMEM((chunks, n - 1, SLOTS, 2, crow, gy), jnp.float32),
         ]
-        + [pltpu.VMEM((SLOTS * n, 2, crow, gy), jnp.float32)] * chunks
+        + [pltpu.VMEM((n - 1, SLOTS, 2, k * gx, gy), jnp.float32) for k in sizes]
+        + [pltpu.VMEM((SLOTS * n, 2, k * gx, gy), jnp.float32) for k in sizes]
         + [
-            pltpu.SemaphoreType.DMA,
-            pltpu.SemaphoreType.DMA((chunks,)),
+            pltpu.SemaphoreType.DMA((3,)),
+            pltpu.SemaphoreType.DMA((len(sizes),)),
             pltpu.SemaphoreType.DMA((8,)),
             pltpu.SemaphoreType.DMA((8,)),
             pltpu.SemaphoreType.DMA((m,)),
             pltpu.SemaphoreType.DMA((m,)),
-            pltpu.SemaphoreType.DMA((chunks, n)),
-            pltpu.SemaphoreType.DMA((chunks, n)),
+            pltpu.SemaphoreType.DMA((len(sizes), n)),
+            pltpu.SemaphoreType.DMA((len(sizes), n)),
         ],
         compiler_params=pltpu.CompilerParams(
-            collective_id=0, has_side_effects=True, vmem_limit_bytes=48 * 1024 * 1024
+            collective_id=0, has_side_effects=True, vmem_limit_bytes=63 * 1024 * 1024
         ),
         cost_estimate=pl.CostEstimate(
             flops=110 * flat.size, bytes_accessed=8 * flat.size, transcendentals=flat.size
         ),
-    )(flat, sources, levels)
+    )(flat, sources.T, levels)
     return moved.reshape(state.shape)
 
 

time: 53.3 us -> 46.9 us (0.88)
  Pallas kernels: 49.3 us -> 44.5 us
  local copies, waits for them, and re-layouts: 3.53 us -> 2.3 us
    pallas_call x1, Pallas kernels: 49.3 us -> 44.5 us  [local(): pl.pallas_call(functools.partial(kernel, n, m, per, depth, gx, sizes), ou...]
    unnamed x8 -> x1, local copies, waits for them, and re-layouts: 3.53 us -> 2.3 us
where the time goes in v2:
time: 46.9 us; the launch traced here: 46.8 us
  Pallas kernels  44.5 us (95%)
  local copies, waits for them, and re-layouts  2.3 us (5%)
    pallas_call x1, Pallas kernels, local(): pl.pallas_call(functools.partial(kernel, n, m, per, depth, gx, sizes), ou...  44.5 us
    unnamed x1, local copies, waits for them, and re-layouts  2.3 us

profile of v2, /device:TPU:0, one launch (start us, length us, event | category | flops | bytes accessed | tf_op | source)
XLA Modules:
  0.0 46.8 jit_solution(14162033681666026389)
XLA Ops:
  0.0 44.5 %shard_map.37 = f32[8,2,128,128]{3,2,1,0:T(8,128)} custom-call(f32[8,2,128,128]{3,2,1,0:T(8,128)} %bitcast.4, s32[2,64]{1,0:T(2,128)} %bitcast.5, s32[8]{0:T(128)} %levels_hbm.1), custom_call_target="tpu_custom_call" | custom-call | flops 28835840 | bytes 2097152 | tf_op jit(solution)/shard_map/pallas_call | solution.py:491
  44.5 2.3 %copy.5 = f32[8,2,32,4,128]{4,3,2,1,0:T(4,128)} copy(f32[8,2,32,4,128]{4,3,2,1,0:T(4,128)} %bitcast.3) | data formatting | bytes 2097152

commit v3 on v2

v3 whole, which is shorter than its diff:
```python
import functools

import jax
import jax.numpy as jnp
from jax import lax
from jax.experimental import pallas as pl
from jax.experimental.pallas import tpu as pltpu
from jax.sharding import PartitionSpec as P

MESH = pl.DeviceIdType.MESH
WLEVELS = 16
KAPPA = 0.25
COUPLE = 0.3
STEP_SIZE = 0.004
EPSILON = 1e-06
SLOTS = 2
HALO = 4
RIM = 2


def kernel(
    n, m, per, depth, gx, chunks,
    state, sources_hbm, levels_hbm, out,
    sources, levels, land, edge, cells, mu_s, hm_s, b_s, t_s, sec_s, r_s, q_s, upd, sums, outbuf,
    pick, where_from, sbuf, *rest,
):
    rbufs = rest[:chunks]
    load_sem, out_sem, hs_sem, hr_sem, ss_sem, sr_sem, as_sem, ar_sem = rest[chunks:]
    me = lax.axis_index("img")
    slab = lax.axis_index("slab")
    entries = per * 2
    images = per * n
    planes = depth + 2 * HALO
    rows = gx * per
    step = depth // chunks
    crow = step * gx
    own = depth * gx

    def rem(a, b):
        return lax.rem(a, jnp.int32(b))

    nxt, prv = rem(me + 1, n), rem(me + n - 1, n)

    def partner(o):
        other, bit = me, 1
        while bit < n:
            flip = rem(lax.div(o, jnp.int32(bit)), 2)
            other = other + flip * (bit - 2 * bit * rem(lax.div(me, jnp.int32(bit)), 2))
            bit *= 2
        return other

    def each(body):
        def one(i, carry):
            body(n - 1 - i)
            return carry

        lax.fori_loop(0, n - 1, one, 0)

    has_low, has_high = slab > 0, slab < m - 1

    def loads():
        return pltpu.make_async_copy(
            state, land.at[:, :, pl.ds(HALO * gx, own), :], load_sem.at[0]
        )

    tables = [
        pltpu.make_async_copy(sources_hbm, sources, load_sem.at[1]),
        pltpu.make_async_copy(levels_hbm, levels, load_sem.at[2]),
    ]
    loads().start()
    for c in tables:
        c.start()

    barrier = pltpu.get_barrier_semaphore()

    def greet(i, s):
        pl.semaphore_signal(
            barrier, inc=1, device_id={"img": i, "slab": s}, device_id_type=MESH
        )

    each(lambda o: greet(partner(o), slab))
    for o in range(1, m):
        greet(me, rem(slab + o, m))

    @pl.when(has_low)
    def _():
        greet(nxt, slab - 1)
        greet(prv, slab - 1)

    @pl.when(has_high)
    def _():
        greet(nxt, slab + 1)
        greet(prv, slab + 1)

    count = (n - 1) + (m - 1) + jnp.where(has_low, 2, 0) + jnp.where(has_high, 2, 0)
    pl.semaphore_wait(barrier, count)
    for c in tables:
        c.wait()

    def halo(k, src, dst, i, s):
        return pltpu.make_async_remote_copy(
            src_ref=src, dst_ref=dst, send_sem=hs_sem.at[k], recv_sem=hr_sem.at[k],
            device_id={"img": i, "slab": s}, device_id_type=MESH,
        )

    hr, rr, top = HALO * gx, RIM * gx, (HALO + depth) * gx
    last = per - 1
    to_high = [
        halo(0, state.at[:, :, pl.ds(own - hr, hr), :], land.at[:, :, pl.ds(0, hr), :], me, slab + 1),
        halo(4, state.at[last, :, pl.ds(own - rr, rr), :], edge.at[0, :, pl.ds(hr - rr, rr), :], nxt, slab + 1),
        halo(5, state.at[0, :, pl.ds(own - rr, rr), :], edge.at[1, :, pl.ds(hr - rr, rr), :], prv, slab + 1),
    ]
    to_low = [
        halo(1, state.at[:, :, pl.ds(0, hr), :], land.at[:, :, pl.ds(top, hr), :], me, slab - 1),
        halo(6, state.at[last, :, pl.ds(0, rr), :], edge.at[0, :, pl.ds(top, rr), :], nxt, slab - 1),
        halo(7, state.at[0, :, pl.ds(0, rr), :], edge.at[1, :, pl.ds(top, rr), :], prv, slab - 1),
    ]
    beside = [
        halo(2, state.at[last], edge.at[0, :, pl.ds(hr, own), :], nxt, slab),
        halo(3, state.at[0], edge.at[1, :, pl.ds(hr, own), :], prv, slab),
    ]

    @pl.when(has_high)
    def _():
        for c in to_high:
            c.start()

    @pl.when(has_low)
    def _():
        for c in to_low:
            c.start()

    for c in beside:
        c.start()

    def rx(a, up):
        k = per if up else rows - per
        return jnp.concatenate([a[k:], a[:k]], axis=0)

    def ry(a, up):
        return pltpu.roll(a, a.shape[1] - 1 if up else 1, 1)

    def at(f, z):
        start = (f * planes + z) * rows
        return pl.ds(start if isinstance(start, int) else pl.multiple_of(start, 8), rows)

    def loop(lo, hi, body, carry, k=2):
        full = (hi - lo) // k
        if full:
            carry = lax.fori_loop(0, full, lambda i, c: body(lo + i * k, c, k), carry)
        if lo + full * k < hi:
            carry = body(lo + full * k, carry, hi - lo - full * k)
        return carry

    def take(ref, z, j0, j1):
        return [{j: ref[at(f, z + j), :] for j in range(j0, j1)} for f in range(2)]

    def give(ref, z, values):
        for f in range(2):
            for j, v in values[f].items():
                ref[at(f, z + j), :] = v

    def settle(lo, hi):
        def body(g, carry):
            for f in range(2):
                for i in range(per):
                    cells[pl.ds((f * planes + 2 * g) * rows + i, 8, stride=per), :] = land[
                        i, f, pl.ds(pl.multiple_of(8 * g, 8), 8), :
                    ]
            return carry

        lax.fori_loop(lo // 2, hi // 2, body, 0)

    def potentials():
        def body(z, carry, k):
            s = take(cells, z, -1, k + 1)
            mu, hm = [{}, {}], [{}, {}]
            for j in range(k):
                for f in range(2):
                    a = s[f][j]
                    sq = a * a
                    near = (s[f][j + 1] + s[f][j - 1]) + (rx(a, True) + rx(a, False))
                    near = near + (ry(a, True) + ry(a, False))
                    mu[f][j] = a * (sq + (6.0 * KAPPA - 1.0)) + COUPLE * s[1 - f][j] - KAPPA * near
                    hm[f][j] = 0.25 + 0.5 / (1.0 + sq)
            give(mu_s, z, mu)
            give(hm_s, z, hm)
            return carry

        return body

    zero = jnp.zeros((rows, 128), jnp.float32)
    loads().wait()
    settle(HALO, HALO + depth)
    potential = potentials()
    loop(HALO + 1, HALO + depth - 1, potential, 0, 3)

    @pl.when(has_low)
    def _():
        for k in range(3):
            halo(0, *((land.at[:, :, pl.ds(0, hr), :],) * 2), me, slab - 1).wait_recv() if k == 0 else \
                halo(3 + k, *((edge.at[k - 1, :, pl.ds(hr - rr, rr), :],) * 2), me, slab - 1).wait_recv()
        settle(0, HALO)

    @pl.when(has_high)
    def _():
        for k in range(3):
            halo(1, *((land.at[:, :, pl.ds(top, hr), :],) * 2), me, slab + 1).wait_recv() if k == 0 else \
                halo(5 + k, *((edge.at[k - 1, :, pl.ds(top, rr), :],) * 2), me, slab + 1).wait_recv()
        settle(HALO + depth, planes)

    @pl.when(jnp.logical_not(has_low))
    def _():
        for f in range(2):
            for z in range(HALO):
                cells[at(f, z), :] = zero
            for k in range(2):
                edge[k, f, pl.ds(hr - rr, rr), :] = zero[:rr]

    @pl.when(jnp.logical_not(has_high))
    def _():
        for f in range(2):
            for z in range(HALO + depth, planes):
                cells[at(f, z), :] = zero
            for k in range(2):
                edge[k, f, pl.ds(top, rr), :] = zero[:rr]

    lax.fori_loop(0, 2, lambda i, c: potential(1 + i * (HALO + depth - 2), c, HALO), 0)

    def mirror(ref):
        @pl.when(jnp.logical_not(has_low))
        def _():
            for f in range(2):
                ref[at(f, HALO - 1), :] = ref[at(f, HALO), :]

        @pl.when(jnp.logical_not(has_high))
        def _():
            for f in range(2):
                ref[at(f, HALO + depth), :] = ref[at(f, HALO + depth - 1), :]

    mirror(mu_s)
    for c in beside:
        c.wait_recv()

    line = lax.broadcasted_iota(jnp.int32, (per, 128), 0)
    at_last = line == per - 1
    at_first = line == 0

    def shifted(a, f, z):
        low, high = [], []
        for x in range(gx):
            tile = a[x * per : (x + 1) * per]
            r = pl.ds(z * gx + x, 1)
            before = jnp.broadcast_to(edge[0, f, r, :], (per, 128))
            after = jnp.broadcast_to(edge[1, f, r, :], (per, 128))
            low.append(pltpu.roll(jnp.where(at_last, before, tile), 1, 0))
            high.append(pltpu.roll(jnp.where(at_first, after, tile), per - 1, 0))
        return jnp.concatenate(low, axis=0), jnp.concatenate(high, axis=0)

    def fold(a):
        total = a[:per]
        for x in range(1, gx):
            total = total + a[x * per : (x + 1) * per]
        return total

    def z_flux(f, z):
        return (hm_s[at(f, z), :] + hm_s[at(f, z + 1), :]) * (mu_s[at(f, z + 1), :] - mu_s[at(f, z), :])

    def drifts(z, carry, k):
        flux, acc_b, acc_t = list(carry[0:2]), carry[2], carry[3]
        hm, mu, s = take(hm_s, z, 0, k + 1), take(mu_s, z, 0, k + 1), take(cells, z, 0, k)
        near = [[shifted(s[f][j], f, z + j) for j in range(k)] for f in range(2)]
        b, t, sec = [{}, {}], [{}, {}], [{}, {}]
        for j in range(k):
            for f in range(2):
                h, u = hm[f][j], mu[f][j]
                fz = (h + hm[f][j + 1]) * (mu[f][j + 1] - u)
                fx = (h + rx(h, True)) * (rx(u, True) - u)
                fy = (h + ry(h, True)) * (ry(u, True) - u)
                b[f][j] = (fz - flux[f]) + (fx - rx(fx, False)) + (fy - ry(fy, False))
                flux[f] = fz
                low, high = near[f][j]
                t[f][j] = (high - low) * ((images - 1) / 2.0)
                sec[f][j] = (high + low - 2.0 * s[f][j]) * float((images - 1) ** 2)
                inside = (z + j >= HALO) & (z + j < HALO + depth)
                counts = jnp.where(inside, jnp.float32(1.0), jnp.float32(0.0))
                acc_b = acc_b + counts * fold(b[f][j] * b[f][j])
                acc_t = acc_t + counts * fold(t[f][j] * t[f][j])
        give(b_s, z, b)
        give(t_s, z, t)
        give(sec_s, z, sec)
        return (flux[0], flux[1], acc_b, acc_t)

    none = jnp.zeros((per, 128), jnp.float32)
    carry = (z_flux(0, HALO - RIM - 1), z_flux(1, HALO - RIM - 1), none, none)
    carry = loop(HALO - RIM, HALO + depth + RIM, drifts, carry, 4)
    sums[0, 0] = carry[2]
    sums[0, 1] = carry[3]

    def share(o):
        return pltpu.make_async_remote_copy(
            src_ref=sums.at[0], dst_ref=sums.at[o], send_sem=ss_sem.at[o], recv_sem=sr_sem.at[o],
            device_id={"img": me, "slab": rem(slab + o, m)}, device_id_type=MESH,
        )

    for o in range(1, m):
        share(o).start()
    mirror(t_s)
    mirror(b_s)

    def choose(d, carry):
        seen = jnp.int32(0)
        first = jnp.int32(0)
        second = jnp.int32(0)
        for e in range(entries):
            src = sources[e % 2, d * per + e // 2]
            mine = lax.div(src, jnp.int32(per)) == me
            place = lax.rem(src, jnp.int32(per))
            first = jnp.where(mine & (seen == 0), place, first)
            second = jnp.where(mine & (seen == 1), place, second)
            seen = seen + jnp.where(mine, 1, 0)
        pick[SLOTS * d] = first
        pick[SLOTS * d + 1] = second
        return carry

    lax.fori_loop(0, n, choose, 0)
    owners = []
    for e in range(entries):
        owner = lax.div(sources[e % 2, me * per + e // 2], jnp.int32(per))
        slot = jnp.int32(0)
        for before in owners:
            slot = jnp.where(before == owner, 1, slot)
        owners.append(owner)
        where_from[e] = SLOTS * owner + slot

    for o in range(1, m):
        share(o).wait_recv()
    total_b, total_t = sums[0, 0], sums[0, 1]
    for o in range(1, m):
        total_b = total_b + sums[o, 0]
        total_t = total_t + sums[o, 1]
    total_b = jnp.sum(total_b, axis=1, keepdims=True)
    total_t = jnp.sum(total_t, axis=1, keepdims=True)
    lam = jnp.sqrt(total_b) / jnp.sqrt(total_t + EPSILON)
    lam = jnp.broadcast_to(lam, (per, 128))
    ids = line + me * per
    inner = jnp.where((ids > 0) & (ids < images - 1), STEP_SIZE, 0.0).astype(jnp.float32)

    def wide(a):
        return jnp.concatenate([a] * gx, axis=0)

    lam_w, inner_w = wide(lam), wide(inner)
    square_w = wide(inner * lam * lam)

    def moment(f, z):
        return lam_w * t_s[at(f, z), :] - b_s[at(f, z), :]

    def adjoint(z, carry, k):
        flux, prod = list(carry[0:2]), list(carry[2:4])
        hm, mu = take(hm_s, z, 0, k + 1), take(mu_s, z, 0, k + 1)
        mo = [{j: moment(f, z + j) for j in range(k + 1)} for f in range(2)]
        r, q = [{}, {}], [{}, {}]
        for j in range(k):
            for f in range(2):
                h, u, o = hm[f][j], mu[f][j], mo[f][j]
                dz, dx, dy = mo[f][j + 1] - o, rx(o, True) - o, ry(o, True) - o
                fz = (h + hm[f][j + 1]) * dz
                fx = (h + rx(h, True)) * dx
                fy = (h + ry(h, True)) * dy
                pz = (mu[f][j + 1] - u) * dz
                px = (rx(u, True) - u) * dx
                py = (ry(u, True) - u) * dy
                r[f][j] = (fz - flux[f]) + (fx - rx(fx, False)) + (fy - ry(fy, False))
                q[f][j] = (pz + prod[f]) + (px + rx(px, False)) + (py + ry(py, False))
                flux[f], prod[f] = fz, pz
        give(r_s, z, r)
        give(q_s, z, q)
        return (flux[0], flux[1], prod[0], prod[1])

    def finish(z, carry, k):
        r, s, hm = take(r_s, z, -1, k + 1), take(cells, z, 0, k), take(hm_s, z, 0, k)
        q, sec = take(q_s, z, 0, k), take(sec_s, z, 0, k)
        new = [{}, {}]
        for j in range(k):
            for f in range(2):
                a, c = s[f][j], r[f][j]
                near = (r[f][j + 1] + r[f][j - 1]) + (rx(c, True) + rx(c, False))
                near = near + (ry(c, True) + ry(c, False))
                inv = 2.0 * hm[f][j] - 0.5
                pulled = (3.0 * (a * a) + (6.0 * KAPPA - 1.0)) * c + COUPLE * r[1 - f][j] - KAPPA * near
                pulled = pulled + (a * inv) * (inv * q[f][j])
                new[f][j] = a + (square_w * sec[f][j] + inner_w * pulled)
        give(upd, z, new)
        return carry

    def pack(dest, c, put):
        for s in range(SLOTS):
            image = pick[SLOTS * dest + s]
            for f in range(2):
                for g in range(crow // 8):
                    start = (f * planes + HALO + c * step) * rows + g * 8 * per
                    put(s, f, pl.ds(8 * g, 8), upd[pl.ds(start + image, 8, stride=per), :])

    def exchange(c, o, to):
        return pltpu.make_async_remote_copy(
            src_ref=sbuf.at[c, o - 1], dst_ref=rbufs[c].at[pl.ds(SLOTS * to, SLOTS)],
            send_sem=as_sem.at[c, o], recv_sem=ar_sem.at[c, o],
            device_id={"img": partner(o), "slab": slab}, device_id_type=MESH,
        )

    first = HALO - 2
    dz = [moment(f, first + 1) - moment(f, first) for f in range(2)]
    carry = tuple(
        [(hm_s[at(f, first), :] + hm_s[at(f, first + 1), :]) * dz[f] for f in range(2)]
        + [(mu_s[at(f, first + 1), :] - mu_s[at(f, first), :]) * dz[f] for f in range(2)]
    )
    carry = adjoint(HALO - 1, carry, 2)

    @pl.when(jnp.logical_not(has_low))
    def _():
        for f in range(2):
            r_s[at(f, HALO - 1), :] = zero

    def chunk(c, carry):
        z = HALO + c * step
        carry = lax.fori_loop(0, step // 2, lambda i, a: adjoint(z + 1 + 2 * i, a, 2), carry)

        @pl.when(jnp.logical_not(has_high) & (c == chunks - 1))
        def _():
            for f in range(2):
                r_s[at(f, HALO + depth), :] = zero

        lax.fori_loop(0, step // 2, lambda i, a: finish(z + 2 * i, a, 2), 0)

        def fill(o):
            def put(s, f, where, value):
                sbuf[c, o - 1, s, f, where, :] = value

            pack(partner(o), c, put)

        each(fill)
        for k in range(chunks):
            @pl.when(c == k)
            def _():
                each(lambda o: exchange(k, o, me).start())

                def keep(s, f, where, value):
                    rbufs[k][SLOTS * me + s, f, where, :] = value

                pack(me, k, keep)

        return carry

    lax.fori_loop(0, chunks, chunk, carry)

    def store(c):
        part = pl.ds(c * crow, crow)
        return pltpu.make_async_copy(outbuf.at[:, :, part, :], out.at[:, :, part, :], out_sem.at[c])

    for c in range(chunks):
        each(lambda o: exchange(c, o, partner(o)).wait_recv())

        def blend(j, carry):
            weight = (levels[j].astype(jnp.float32) + 1.0) * (1.0 / (WLEVELS + 1.0))
            one, two = where_from[2 * j], where_from[2 * j + 1]
            for f in range(2):
                outbuf[j, f, pl.ds(c * crow, crow), :] = (
                    weight * rbufs[c][one, f] + (1.0 - weight) * rbufs[c][two, f]
                )
            return carry

        lax.fori_loop(0, per, blend, 0)
        store(c).start()

    for c in range(chunks):
        each(lambda o: exchange(c, o, me).wait_send())
        store(c).wait()
    for o in range(1, m):
        share(o).wait_send()
    for c in beside:
        c.wait_send()

    @pl.when(has_high)
    def _():
        for c in to_high:
            c.wait_send()

    @pl.when(has_low)
    def _():
        for c in to_low:
            c.wait_send()


def local(n, m, state, sources, levels):
    per, _, depth, gx, gy = state.shape
    planes = depth + 2 * HALO
    chunks = depth // 4
    crow = depth // chunks * gx
    field = pltpu.VMEM((2 * planes * gx * per, gy), jnp.float32)
    flat = state.reshape(per, 2, depth * gx, gy)
    moved = pl.pallas_call(
        functools.partial(kernel, n, m, per, depth, gx, chunks),
        out_shape=jax.ShapeDtypeStruct(flat.shape, jnp.float32),
        in_specs=[pl.BlockSpec(memory_space=pltpu.HBM)] * 3,
        out_specs=pl.BlockSpec(memory_space=pl.ANY),
        scratch_shapes=[
            pltpu.SMEM((2, n * per), jnp.int32),
            pltpu.SMEM((per,), jnp.int32),
            pltpu.VMEM((per, 2, planes * gx, gy), jnp.float32),
            pltpu.VMEM((2, 2, planes * gx, gy), jnp.float32),
        ]
        + [field] * 9
        + [
            pltpu.VMEM((m, 2, per, gy), jnp.float32),
            pltpu.VMEM((per, 2, depth * gx, gy), jnp.float32),
            pltpu.SMEM((SLOTS * n,), jnp.int32),
            pltpu.SMEM((2 * per,), jnp.int32),
        ]
        + [pltpu.VMEM((chunks, n - 1, SLOTS, 2, crow, gy), jnp.float32)]
        + [pltpu.VMEM((SLOTS * n, 2, crow, gy), jnp.float32)] * chunks
        + [
            pltpu.SemaphoreType.DMA((3,)),
            pltpu.SemaphoreType.DMA((chunks,)),
            pltpu.SemaphoreType.DMA((8,)),
            pltpu.SemaphoreType.DMA((8,)),
            pltpu.SemaphoreType.DMA((m,)),
            pltpu.SemaphoreType.DMA((m,)),
            pltpu.SemaphoreType.DMA((chunks, n)),
            pltpu.SemaphoreType.DMA((chunks, n)),
        ],
        compiler_params=pltpu.CompilerParams(
            collective_id=0, has_side_effects=True, vmem_limit_bytes=48 * 1024 * 1024
        ),
        cost_estimate=pl.CostEstimate(
            flops=110 * flat.size, bytes_accessed=8 * flat.size, transcendentals=flat.size
        ),
    )(*(pltpu.with_memory_space_constraint(x, pltpu.HBM) for x in (flat, sources.T, levels)))
    return moved.reshape(state.shape)


def solution(mesh):
    return jax.shard_map(
        functools.partial(local, mesh.shape["img"], mesh.shape["slab"]),
        mesh=mesh,
        in_specs=(P("img", None, "slab", None, None), P(), P("img")),
        out_specs=P("img", None, "slab", None, None),
        check_vma=False,
    )
```

time: 46.9 us -> 45.1 us (0.962)
  local copies, waits for them, and re-layouts: 2.3 us -> 0.97 us
  Pallas kernels: 44.5 us -> 43.9 us
    unnamed x1, local copies, waits for them, and re-layouts: 2.3 us -> 0.97 us
    pallas_call x1, Pallas kernels: 44.5 us -> 43.9 us  [local(): pl.pallas_call(functools.partial(kernel, n, m, per, depth, gx, chunks), o...]
where the time goes in v3:
time: 45.1 us; the launch traced here: 44.9 us
  Pallas kernels  43.9 us (97%)
  local copies, waits for them, and re-layouts  0.97 us (2%)
    pallas_call x1, Pallas kernels, local(): pl.pallas_call(functools.partial(kernel, n, m, per, depth, gx, chunks), o...  43.9 us
    unnamed x1, local copies, waits for them, and re-layouts  0.97 us

profile of v3, /device:TPU:0, one launch (start us, length us, event | category | flops | bytes accessed | tf_op | source)
XLA Modules:
  0.0 44.9 jit_solution(6694739007523695089)
XLA Ops:
  0.0 43.9 %shard_map.37 = f32[8,2,128,128]{3,2,1,0:T(8,128)S(1)} custom-call(f32[8,2,128,128]{3,2,1,0:T(8,128)} %bitcast.4, s32[2,64]{1,0:T(2,128)} %bitcast.5, s32[8]{0:T(128)} %levels_hbm.1), custom_call_target="tpu_custom_call" | custom-call | flops 28835840 | bytes 2097152 | tf_op jit(solution)/shard_map/pallas_call | solution.py:501
  43.9 1.0 %copy.5 = f32[8,2,32,4,128]{4,3,2,1,0:T(4,128)} copy(f32[8,2,32,4,128]{4,3,2,1,0:T(4,128)S(1)} %bitcast.3) | data formatting | bytes 2097152

commit v4 on v3

--- a/solution.py
+++ b/solution.py
@@ -41,12 +41,13 @@
 
     nxt, prv = rem(me + 1, n), rem(me + n - 1, n)
 
+    bits = [1 << k for k in range(n.bit_length() - 1)]
+    turns = [bit - 2 * bit * rem(lax.div(me, jnp.int32(bit)), 2) for bit in bits]
+
     def partner(o):
-        other, bit = me, 1
-        while bit < n:
-            flip = rem(lax.div(o, jnp.int32(bit)), 2)
-            other = other + flip * (bit - 2 * bit * rem(lax.div(me, jnp.int32(bit)), 2))
-            bit *= 2
+        other = me
+        for bit, turn in zip(bits, turns):
+            other = other + rem(lax.div(o, jnp.int32(bit)), 2) * turn
         return other
 
     def each(body):
@@ -93,6 +94,19 @@
         greet(prv, slab + 1)
 
     count = (n - 1) + (m - 1) + jnp.where(has_low, 2, 0) + jnp.where(has_high, 2, 0)
+    def settle(lo, hi):
+        def body(g, carry):
+            for f in range(2):
+                for i in range(per):
+                    cells[pl.ds((f * planes + 2 * g) * rows + i, 8, stride=per), :] = land[
+                        i, f, pl.ds(pl.multiple_of(8 * g, 8), 8), :
+                    ]
+            return carry
+
+        lax.fori_loop(lo // 2, hi // 2, body, 0)
+
+    loads().wait()
+    settle(HALO, HALO + depth)
     pl.semaphore_wait(barrier, count)
     for c in tables:
         c.wait()
@@ -160,17 +174,6 @@
             for j, v in values[f].items():
                 ref[at(f, z + j), :] = v
 
-    def settle(lo, hi):
-        def body(g, carry):
-            for f in range(2):
-                for i in range(per):
-                    cells[pl.ds((f * planes + 2 * g) * rows + i, 8, stride=per), :] = land[
-                        i, f, pl.ds(pl.multiple_of(8 * g, 8), 8), :
-                    ]
-            return carry
-
-        lax.fori_loop(lo // 2, hi // 2, body, 0)
-
     def potentials():
         def body(z, carry, k):
             s = take(cells, z, -1, k + 1)
@@ -190,8 +193,6 @@
         return body
 
     zero = jnp.zeros((rows, 128), jnp.float32)
-    loads().wait()
-    settle(HALO, HALO + depth)
     potential = potentials()
     loop(HALO + 1, HALO + depth - 1, potential, 0, 3)
 
@@ -432,17 +433,17 @@
 
         lax.fori_loop(0, step // 2, lambda i, a: finish(z + 2 * i, a, 2), 0)
 
-        def fill(o):
-            def put(s, f, where, value):
-                sbuf[c, o - 1, s, f, where, :] = value
-
-            pack(partner(o), c, put)
-
-        each(fill)
         for k in range(chunks):
             @pl.when(c == k)
             def _():
-                each(lambda o: exchange(k, o, me).start())
+                def ship(o):
+                    def put(s, f, where, value):
+                        sbuf[k, o - 1, s, f, where, :] = value
+
+                    pack(partner(o), k, put)
+                    exchange(k, o, me).start()
+
+                each(ship)
 
                 def keep(s, f, where, value):
                     rbufs[k][SLOTS * me + s, f, where, :] = value

time: 45.1 us -> 44.9 us (level)
  no operation moved by 1% of the time
where the time goes in v4:
time: 44.9 us; the launch traced here: 44.7 us
  Pallas kernels  43.8 us (98%)
  local copies, waits for them, and re-layouts  0.97 us (2%)
    pallas_call x1, Pallas kernels, local(): pl.pallas_call(functools.partial(kernel, n, m, per, depth, gx, chunks), o...  43.8 us
    unnamed x1, local copies, waits for them, and re-layouts  0.97 us

profile of v4, /device:TPU:0, one launch (start us, length us, event | category | flops | bytes accessed | tf_op | source)
XLA Modules:
  0.0 44.7 jit_solution(5319303391639697990)
XLA Ops:
  0.0 43.8 %shard_map.37 = f32[8,2,128,128]{3,2,1,0:T(8,128)S(1)} custom-call(f32[8,2,128,128]{3,2,1,0:T(8,128)} %bitcast.4, s32[2,64]{1,0:T(2,128)} %bitcast.5, s32[8]{0:T(128)} %levels_hbm.1), custom_call_target="tpu_custom_call" | custom-call | flops 28835840 | bytes 2097152 | tf_op jit(solution)/shard_map/pallas_call | solution.py:502
  43.8 1.0 %copy.5 = f32[8,2,32,4,128]{4,3,2,1,0:T(4,128)} copy(f32[8,2,32,4,128]{4,3,2,1,0:T(4,128)S(1)} %bitcast.3) | data formatting | bytes 2097152

commit v5 on v4

--- a/solution.py
+++ b/solution.py
@@ -105,8 +105,6 @@
 
         lax.fori_loop(lo // 2, hi // 2, body, 0)
 
-    loads().wait()
-    settle(HALO, HALO + depth)
     pl.semaphore_wait(barrier, count)
     for c in tables:
         c.wait()
@@ -134,6 +132,9 @@
         halo(3, state.at[0], edge.at[1, :, pl.ds(hr, own), :], prv, slab),
     ]
 
+    for c in beside:
+        c.start()
+
     @pl.when(has_high)
     def _():
         for c in to_high:
@@ -143,9 +144,6 @@
     def _():
         for c in to_low:
             c.start()
-
-    for c in beside:
-        c.start()
 
     def rx(a, up):
         k = per if up else rows - per
@@ -193,40 +191,10 @@
         return body
 
     zero = jnp.zeros((rows, 128), jnp.float32)
+    loads().wait()
+    settle(HALO, HALO + depth)
     potential = potentials()
     loop(HALO + 1, HALO + depth - 1, potential, 0, 3)
-
-    @pl.when(has_low)
-    def _():
-        for k in range(3):
-            halo(0, *((land.at[:, :, pl.ds(0, hr), :],) * 2), me, slab - 1).wait_recv() if k == 0 else \
-                halo(3 + k, *((edge.at[k - 1, :, pl.ds(hr - rr, rr), :],) * 2), me, slab - 1).wait_recv()
-        settle(0, HALO)
-
-    @pl.when(has_high)
-    def _():
-        for k in range(3):
-            halo(1, *((land.at[:, :, pl.ds(top, hr), :],) * 2), me, slab + 1).wait_recv() if k == 0 else \
-                halo(5 + k, *((edge.at[k - 1, :, pl.ds(top, rr), :],) * 2), me, slab + 1).wait_recv()
-        settle(HALO + depth, planes)
-
-    @pl.when(jnp.logical_not(has_low))
-    def _():
-        for f in range(2):
-            for z in range(HALO):
-                cells[at(f, z), :] = zero
-            for k in range(2):
-                edge[k, f, pl.ds(hr - rr, rr), :] = zero[:rr]
-
-    @pl.when(jnp.logical_not(has_high))
-    def _():
-        for f in range(2):
-            for z in range(HALO + depth, planes):
-                cells[at(f, z), :] = zero
-            for k in range(2):
-                edge[k, f, pl.ds(top, rr), :] = zero[:rr]
-
-    lax.fori_loop(0, 2, lambda i, c: potential(1 + i * (HALO + depth - 2), c, HALO), 0)
 
     def mirror(ref):
         @pl.when(jnp.logical_not(has_low))
@@ -239,7 +207,6 @@
             for f in range(2):
                 ref[at(f, HALO + depth), :] = ref[at(f, HALO + depth - 1), :]
 
-    mirror(mu_s)
     for c in beside:
         c.wait_recv()
 
@@ -293,8 +260,50 @@
         return (flux[0], flux[1], acc_b, acc_t)
 
     none = jnp.zeros((per, 128), jnp.float32)
-    carry = (z_flux(0, HALO - RIM - 1), z_flux(1, HALO - RIM - 1), none, none)
-    carry = loop(HALO - RIM, HALO + depth + RIM, drifts, carry, 4)
+    def along(z, acc):
+        return (z_flux(0, z - 1), z_flux(1, z - 1)) + acc
+
+    carry = loop(HALO + 2, HALO + depth - 2, drifts, along(HALO + 2, (none, none)), 4)
+
+    @pl.when(has_low)
+    def _():
+        for k in range(3):
+            halo(0, *((land.at[:, :, pl.ds(0, hr), :],) * 2), me, slab - 1).wait_recv() if k == 0 else \
+                halo(3 + k, *((edge.at[k - 1, :, pl.ds(hr - rr, rr), :],) * 2), me, slab - 1).wait_recv()
+        settle(0, HALO)
+
+    @pl.when(has_high)
+    def _():
+        for k in range(3):
+            halo(1, *((land.at[:, :, pl.ds(top, hr), :],) * 2), me, slab + 1).wait_recv() if k == 0 else \
+                halo(5 + k, *((edge.at[k - 1, :, pl.ds(top, rr), :],) * 2), me, slab + 1).wait_recv()
+        settle(HALO + depth, planes)
+
+    @pl.when(jnp.logical_not(has_low))
+    def _():
+        for f in range(2):
+            for z in range(HALO):
+                cells[at(f, z), :] = zero
+            for k in range(2):
+                edge[k, f, pl.ds(hr - rr, rr), :] = zero[:rr]
+
+    @pl.when(jnp.logical_not(has_high))
+    def _():
+        for f in range(2):
+            for z in range(HALO + depth, planes):
+                cells[at(f, z), :] = zero
+            for k in range(2):
+                edge[k, f, pl.ds(top, rr), :] = zero[:rr]
+
+    lax.fori_loop(0, 2, lambda i, c: potential(1 + i * (HALO + depth - 2), c, HALO), 0)
+
+    mirror(mu_s)
+
+    def outer(i, acc):
+        z = HALO - 2 + i * depth
+        return drifts(z, along(z, acc), 4)[2:]
+
+    carry = (None, None) + lax.fori_loop(0, 2, outer, carry[2:])
     sums[0, 0] = carry[2]
     sums[0, 1] = carry[3]
 

time: 44.9 us -> 44.2 us (0.984)
  Pallas kernels: 43.8 us -> 43.1 us
    pallas_call x1, Pallas kernels: 43.8 us -> 43.1 us  [local(): pl.pallas_call(functools.partial(kernel, n, m, per, depth, gx, chunks), o...]
where the time goes in v5:
time: 44.2 us; the launch traced here: 44.1 us
  Pallas kernels  43.1 us (98%)
  local copies, waits for them, and re-layouts  0.97 us (2%)
    pallas_call x1, Pallas kernels, local(): pl.pallas_call(functools.partial(kernel, n, m, per, depth, gx, chunks), o...  43.1 us
    unnamed x1, local copies, waits for them, and re-layouts  0.97 us

profile of v5, /device:TPU:0, one launch (start us, length us, event | category | flops | bytes accessed | tf_op | source)
XLA Modules:
  0.0 44.1 jit_solution(4165306567137684985)
XLA Ops:
  0.0 43.1 %shard_map.37 = f32[8,2,128,128]{3,2,1,0:T(8,128)S(1)} custom-call(f32[8,2,128,128]{3,2,1,0:T(8,128)} %bitcast.4, s32[2,64]{1,0:T(2,128)} %bitcast.5, s32[8]{0:T(128)} %levels_hbm.1), custom_call_target="tpu_custom_call" | custom-call | flops 28835840 | bytes 2097152 | tf_op jit(solution)/shard_map/pallas_call | solution.py:511
  43.1 1.0 %copy.5 = f32[8,2,32,4,128]{4,3,2,1,0:T(4,128)} copy(f32[8,2,32,4,128]{4,3,2,1,0:T(4,128)S(1)} %bitcast.3) | data formatting | bytes 2097152
